TPU v7x, 128 devices: a whole 4x4x4 slice. The times are simulated.
128 devices in a mesh: ctx: 32 (over z, x, y_lo), tp: 4 (over y_hi, core).
Axes of the slice: x: 4, y: 4 (y_hi: 2, y_lo: 2; y = y_hi * 2 + y_lo), z: 4, core: 2. Of those that a mesh axis runs over, the one named last changes fastest.
Arguments:
- queries: bfloat16 [16384, 2048], P('ctx', 'tp'), may hold values from -40 to 40
- keys: bfloat16 [16384, 2048], P('ctx', 'tp'), may hold values from -40 to 40
- values: bfloat16 [16384, 2048], P('ctx', 'tp'), may hold values from -6 to 6
- out_weight: bfloat16 [2048, 4096], P('tp'), may hold values from -0.1875 to 0.1875
- doc_lengths: int32 [64], replicated, may hold values from 1 to 2048, 16384 in all
- layout: int32 [64], replicated, may hold values from 0 to 63, each once
Outputs:
- mixed: bfloat16 [16384, 4096], P('ctx', 'tp')
- log_totals: float32 [16, 16384], P('tp', 'ctx')
Inputs may be any that keep to these rules, and one draw needn't show every extreme that they name: `layout`: every block number appears once. `doc_lengths`: the lengths sum to 16384; the longest is exactly 2048.
All inputs are finite; a program needn't handle non-finite values.
Results may differ from a plain program's by a relative error of at most 0.012.
Values may be sent and summed in bfloat16 or wider, within the bound.
A program may use at most 192 MiB of HBM per device.

v0:
```python
import math

import jax
import jax.numpy as jnp
from jax import lax
from jax.sharding import PartitionSpec as P

HEAD_DIM = 128
LONGEST = 2048


def in_one_piece(arrays, axis, split_dim, concat_dim, along):
    both = jnp.concatenate(arrays, axis=along)
    result, at, gathered = (
        lax.all_to_all(both, axis, split_axis=split_dim, concat_axis=concat_dim, tiled=True),
        0,
        [],
    )
    for a in arrays:
        gathered.append(lax.slice_in_dim(result, at, at + a.shape[along], axis=along))
        at += a.shape[along]
    return tuple(gathered)


def cut_along(array, dim, count):
    before, after = (array.shape[:dim], array.shape[dim + 1 :])
    return jnp.moveaxis(array.reshape(*before, count, -1, *after), dim, 0)


def sum_at_owner(array, axis, dim):
    tiles = cut_along(array, dim, lax.axis_size(axis))
    arrived = lax.all_to_all(tiles, axis, split_axis=0, concat_axis=0, tiled=True)
    return arrived.astype(jnp.float32).sum(axis=0)


def positions_of(layout, first_row, count, half):
    rows = first_row + jnp.arange(count, dtype=jnp.int32)
    block_ids = rows // half
    table = jnp.arange(layout.shape[0], dtype=jnp.int32)
    owner = jnp.sum(jnp.where(block_ids[:, None] == table[None, :], layout[None, :], 0), axis=1)
    return owner * half + rows % half


def documents_of(starts, position):
    return jnp.sum((starts[None, :] <= position[:, None]).astype(jnp.int32), axis=1) - 1


def visible(key_block, key_end_doc, query_block, query_start_doc):
    return (key_block <= query_block) & (
        (key_block == query_block) | (key_end_doc >= query_start_doc)
    )


def local(queries, keys, values, out_weight, doc_lengths, layout):
    rows = queries.shape[0]
    half = rows // 2
    heads = queries.shape[1] // HEAD_DIM
    columns = queries.shape[1]
    scale = 1.0 / math.sqrt(HEAD_DIM)
    starts = jnp.cumsum(doc_lengths) - doc_lengths
    query_pos = positions_of(layout, lax.axis_index("ctx") * rows, rows, half)
    query_doc = documents_of(starts, query_pos)
    query_heads = queries.reshape(rows, heads, HEAD_DIM)

    def update(carry, key_blk, value_blk, allowed):
        top, totals, summed = carry
        scores = (
            jnp.einsum("qhd,khd->hqk", query_heads, key_blk, preferred_element_type=jnp.float32)
            * scale
        )
        scores = jnp.where(allowed[None], scores, -1e30)
        new_top = jnp.maximum(top, jnp.max(scores, axis=-1))
        weights = jnp.where(allowed[None], jnp.exp(scores - new_top[..., None]), 0.0)
        factor = jnp.exp(top - new_top)
        totals = totals * factor + jnp.sum(weights, axis=-1)
        summed = summed * factor.T[:, :, None] + jnp.einsum(
            "hqk,khd->qhd",
            weights.astype(jnp.bfloat16),
            value_blk,
            preferred_element_type=jnp.float32,
        )
        return (new_top, totals, summed)

    def tile(state, key_blk, value_blk, key_pos):
        key_doc = documents_of(starts, key_pos)
        allowed = (key_doc[None, :] == query_doc[:, None]) & (
            key_pos[None, :] <= query_pos[:, None]
        )
        return lax.cond(
            jnp.any(allowed),
            lambda inner: update(inner, key_blk, value_blk, allowed),
            lambda inner: inner,
            state,
        )

    initial = (
        jnp.full((heads, rows), -1e30, jnp.float32),
        jnp.zeros((heads, rows), jnp.float32),
        jnp.zeros((rows, heads, HEAD_DIM), jnp.float32),
    )
    ndevices = lax.axis_size("ctx")
    own = lax.dynamic_slice_in_dim(layout, lax.axis_index("ctx") * 2, 2, 0)
    targets = layout.reshape(ndevices, 2)
    target_docs = documents_of(starts, layout * half).reshape(ndevices, 2)
    own_end = documents_of(starts, own * half + half - 1)
    wanted = visible(
        own[None, :, None], own_end[None, :, None], targets[:, None, :], target_docs[:, None, :]
    )
    wanted = jnp.any(wanted, axis=2)
    key_send = jnp.where(
        wanted[:, :, None, None], keys.reshape(1, 2, half, columns), jnp.zeros((), keys.dtype)
    ).reshape(ndevices * rows, columns)
    value_send = jnp.where(
        wanted[:, :, None, None], values.reshape(1, 2, half, columns), jnp.zeros((), values.dtype)
    ).reshape(ndevices * rows, columns)
    key_got, value_got = in_one_piece((key_send, value_send), "ctx", 0, 0, 1)
    own_start = documents_of(starts, own * half)
    block_end = documents_of(starts, layout * half + half - 1)
    mine = jnp.any(
        visible(layout[:, None], block_end[:, None], own[None, :], own_start[None, :]), axis=1
    )
    count_all = layout.shape[0]
    capacity = min(2 * (LONGEST // half) + 2, count_all)
    ranking = jnp.where(mine, 0, count_all) + jnp.arange(count_all, dtype=jnp.int32)
    order = jnp.argsort(ranking)[:capacity]
    key_slots = key_got.reshape(count_all, half, columns)[order]
    value_slots = value_got.reshape(count_all, half, columns)[order]
    slot_blocks = layout[order]

    def one_slot(index, state):
        key_blk = lax.dynamic_index_in_dim(key_slots, index, 0, keepdims=False).reshape(
            half, heads, HEAD_DIM
        )
        value_blk = lax.dynamic_index_in_dim(value_slots, index, 0, keepdims=False).reshape(
            half, heads, HEAD_DIM
        )
        block_id = lax.dynamic_index_in_dim(slot_blocks, index, 0, keepdims=False)
        key_pos = block_id * half + jnp.arange(half, dtype=jnp.int32)
        return tile(state, key_blk, value_blk, key_pos)

    top, totals, summed = lax.fori_loop(0, capacity, one_slot, initial)
    attended = (summed / totals.T[:, :, None]).reshape(rows, heads * HEAD_DIM).astype(jnp.bfloat16)
    log_totals = top + jnp.log(totals)
    partial_value = jnp.dot(attended, out_weight, preferred_element_type=jnp.float32)
    mixed = sum_at_owner(partial_value.astype(jnp.bfloat16), "tp", 1).astype(jnp.bfloat16)
    return (mixed, log_totals)


def solution(mesh):
    placed = (P("ctx", "tp"), P("ctx", "tp"), P("ctx", "tp"), P("tp", None), P(), P())
    return jax.shard_map(
        local,
        mesh=mesh,
        in_specs=placed,
        out_specs=(P("ctx", "tp"), P("tp", "ctx")),
        check_vma=False,
    )
```

profile of v0, /device:TPU:32, one launch (start us, length us, event | category | flops | bytes accessed | tf_op | source)
XLA Modules:
  0.0 841.9 jit_solution(18029683109873378104)
XLA Ops:
  5.4 12.0 %broadcast_select_fusion.1 = (bf16[32,512,512]{2,1,0:T(8,128)(2,1)}, bf16[32,512,512]{2,1,0:T(8,128)(2,1)}) fusion(pred[32,512]{1,0:T(8,128)(4,1)S(1)} %bitcast.53, bf16[512,512]{1,0:T(8,128)(2,1)} %param.11, bf16[512,512]{1,0:T(8,128)(2,1)} %param.12), kind=kLoop, calls=%fused_computation.29 | loop fusion | flops 16777216 | bytes 34619392 | tf_op jit(solution)/shard_map/jit(_where)/select_n | solution.py:110
  17.4 22.7 %pad_maximum_fusion = bf16[32,512,1024]{2,1,0:T(8,128)(2,1)} fusion(bf16[32,512,512]{2,1,0:T(8,128)(2,1)} %get-tuple-element.447, bf16[32,512,512]{2,1,0:T(8,128)(2,1)} %get-tuple-element.446), kind=kLoop, calls=%fused_computation.27 | loop fusion | flops 67108864 | bytes 67108864 | tf_op jit(solution)/shard_map/concatenate | solution.py:13
  40.1 9.2 %all-to-all-start = ((bf16[32,512,1024]{2,1,0:T(8,128)(2,1)}), bf16[32,512,1024]{2,1,0:T(8,128)(2,1)}, u32[]{:S(2)}, u32[]{:S(2)}) async-start(bf16[32,512,1024]{2,1,0:T(8,128)(2,1)} %pad_maximum_fusion), calls=%async_computation | async-start | bytes 67108864 | tf_op jit(solution)/shard_map/all_to_all | solution.py:15
  49.5 2.0 sort.17
  53.0 595.1 %all-to-all-done = bf16[32,512,1024]{2,1,0:T(8,128)(2,1)} async-done(((bf16[32,512,1024]{2,1,0:T(8,128)(2,1)}), bf16[32,512,1024]{2,1,0:T(8,128)(2,1)}, u32[]{:S(2)}, u32[]{:S(2)}) %all-to-all-start) | async-done | bytes 33554464 | tf_op jit(solution)/shard_map/all_to_all | solution.py:15
  648.1 22.5 %fusion.21 = (bf16[16384,512]{1,0:T(8,128)(2,1)}, bf16[16384,512]{1,0:T(8,128)(2,1)}) fusion(bf16[16384,1024]{1,0:T(8,128)(2,1)} %bitcast.7), kind=kLoop, calls=%fused_computation.69 | loop fusion | bytes 67108864 | tf_op jit(solution)/shard_map/slice | solution.py:20
  670.5 9.7 %gather_fusion.2 = bf16[18,256,512]{2,1,0:T(8,128)(2,1)} fusion(bf16[64,256,512]{2,1,0:T(8,128)(2,1)} %bitcast.44, s32[1024]{0:T(1024)S(1)} %pad_clamp_fusion), kind=kCustom, calls=%fused_computation.2 | custom fusion | bytes 9437256 | tf_op jit(solution)/shard_map/gather | solution.py:127
  680.3 6.6 copy.46
  686.9 9.8 %gather_fusion.1 = bf16[18,256,512]{2,1,0:T(8,128)(2,1)} fusion(bf16[64,256,512]{2,1,0:T(8,128)(2,1)} %bitcast.43, s32[1024]{0:T(1024)S(1)} %pad_clamp_fusion), kind=kCustom, calls=%fused_computation.1 | custom fusion | bytes 9437256 | tf_op jit(solution)/shard_map/gather | solution.py:126
  696.7 6.7 copy.44
  703.5 71.9 %while.19 = (s32[]{:T(128)}, f32[4,512]{1,0:T(4,128)S(1)}, f32[4,512]{1,0:T(4,128)S(1)}, f32[512,4,128]{2,0,1:T(8,128)S(1)}, s32[64]{0:T(128)S(1)}, /*index=5*/s...) while((s32[]{:T(128)}, f32[4,512]{1,0:T(4,128)S(1)}, ...), condition=%wide.region_17.18_spmd, body=%wide.region_10.17_spmd.sunk | while | flops 276355328 | bytes 11152923 | solution.py:141
  706.3 3.4 conditional.2
  706.3 1.1 constant_dynamic-slice_fusion
  708.6 1.1 fusion.3
  712.6 3.4 conditional.2
  712.6 1.1 constant_dynamic-slice_fusion
  714.8 1.1 fusion.3
  718.8 3.4 conditional.2
  718.8 1.1 constant_dynamic-slice_fusion
  721.1 1.1 fusion.3
  725.1 3.4 conditional.2
  725.1 1.1 constant_dynamic-slice_fusion
  727.4 1.1 fusion.3
  731.3 3.4 conditional.2
  733.6 1.1 fusion.3
  737.6 3.4 conditional.2
  739.9 1.1 fusion.3
  775.9 4.6 convolution_convert_fusion
  780.5 2.4 copy.55
  782.9 4.9 all-to-all-start.1
  788.4 49.1 %all-to-all-done.1 = bf16[4,512,1024]{2,1,0:T(8,128)(2,1)} async-done(((bf16[4,512,1024]{2,1,0:T(8,128)(2,1)}), bf16[4,512,1024]{2,1,0:T(8,128)(2,1)}, u32[]{:S(2)}, u32[]{:S(2)}) %all-to-all-start.1) | async-done | bytes 4194336 | tf_op jit(solution)/shard_map/all_to_all | solution.py:32
  837.5 4.4 reduce_sum.99
  (176 shorter events, 44.0 us)
Async XLA Ops:
  40.1 9.3 %copy-start = (s32[64]{0:T(128)S(1)}, s32[64]{0:T(128)}, u32[]{:S(2)}) copy-start(s32[64]{0:T(128)} %param.15) | copy-start | bytes 772
  40.1 12.1 %copy-start.1 = (bf16[512,512]{1,0:T(8,128)(2,1)S(1)}, bf16[512,512]{1,0:T(8,128)(2,1)}, u32[]{:S(2)}) copy-start(bf16[512,512]{1,0:T(8,128)(2,1)} %param.10) | copy-start | bytes 1572868
  40.1 608.0 %all-to-all-start = ((bf16[32,512,1024]{2,1,0:T(8,128)(2,1)}), bf16[32,512,1024]{2,1,0:T(8,128)(2,1)}, u32[]{:S(2)}, u32[]{:S(2)}) async-start(bf16[32,512,1024]{2,1,0:T(8,128)(2,1)} %pad_maximum_fusion), calls=%async_computation | async-start | bytes 67108864 | tf_op jit(solution)/shard_map/all_to_all | solution.py:15
  782.9 54.6 %all-to-all-start.1 = ((bf16[4,512,1024]{2,1,0:T(8,128)(2,1)}), bf16[4,512,1024]{2,1,0:T(8,128)(2,1)}, u32[]{:S(2)}, u32[]{:S(2)}) async-start(bf16[4,512,1024]{2,1,0:T(8,128)(2,1)} %bitcast.46), calls=%async_computation.1 | async-start | bytes 8388608 | tf_op jit(solution)/shard_map/all_to_all | solution.py:32
where the time goes:
time: 843 us; the launch traced here: 842 us
  waiting for transfers between devices  644 us (76%)
  local copies, waits for them, and re-layouts  78.3 us (9%)
  other arithmetic  65 us (8%)
  loops' own time  24.6 us (3%)
  matrix products  14.8 us (2%)
  starting transfers between devices  14.1 us (2%)
    all_to_all x1, waiting for transfers between devices, in_one_piece(): lax.all_to_all(both, axis, split_axis=split_dim, concat_axis=concat_dim,...  595 us
    all_to_all x1, waiting for transfers between devices, sum_at_owner(): lax.all_to_all(tiles, axis, split_axis=0, concat_axis=0, tiled=True)  49.1 us
    another operation x1, loops' own time, local(): top, totals, summed = lax.fori_loop(0, capacity, one_slot, initial)  24.1 us
    concatenate x1, other arithmetic, in_one_piece(): both = jnp.concatenate(arrays, axis=along)  22.7 us
    slice x1, local copies, waits for them, and re-layouts, in_one_piece(): lax.slice_in_dim(result, at, at + a.shape[along], axis=along)  22.5 us
  transfers between devices with their start and end apart: 2, of which 2 were waited for; matrix products, arithmetic and copies ran while one was open for 0% of the time, Pallas kernels for 0%

commit v1 on v0

v1 whole, which is shorter than its diff:
```python
import math

import jax
import jax.numpy as jnp
from jax import lax
from jax.experimental import pallas as pl
from jax.experimental.pallas import tpu as pltpu
from jax.sharding import PartitionSpec as P

HEAD = 128
MESH = pl.DeviceIdType.MESH
ORDER = (0, 1, 3, 2)
LOG2E = math.log2(math.e)


def ctx_of(core, s, r, y):
    return s * (8 - 6 * core) + r * (2 + 6 * core) + y


def my_place():
    ctx, tp = lax.axis_index("ctx"), lax.axis_index("tp")
    z, x, y = lax.div(ctx, 8), lax.rem(lax.div(ctx, 2), 4), lax.rem(ctx, 2)
    core, high = lax.rem(tp, 2), lax.div(tp, 2)
    s = z * (1 - core) + x * core
    r = x * (1 - core) + z * core
    return tp, core, high, s, r, y


def head_columns(s):
    return pl.ds(pl.multiple_of(s * HEAD, HEAD), HEAD)


def gather_kernel(q, k, v, qh, kv, own_sem, s_send, s_recv, g_send, g_recv):
    tp, core, high, s, r, y = my_place()
    left, right, other = lax.rem(r + 3, 4), lax.rem(r + 1, 4), 1 - y
    g_me = r * 2 + y

    def device(s_, r_, y_):
        return (ctx_of(core, s_, r_, y_), tp)

    def spread_from(i):
        return lax.rem(s + 4 - i, 4)

    barrier = pltpu.get_barrier_semaphore()
    partners = [device(lax.rem(s + i, 4), r, y) for i in (1, 2, 3)]
    partners += [device(s, left, y), device(s, right, y), device(s, r, other)]
    for partner in partners:
        pl.semaphore_signal(barrier, inc=1, device_id=partner, device_id_type=MESH)

    own = [
        pltpu.make_async_copy(k.at[:, head_columns(s)], kv.at[g_me, s, 0], own_sem.at[0]),
        pltpu.make_async_copy(v.at[:, head_columns(s)], kv.at[g_me, s, 1], own_sem.at[1]),
        pltpu.make_async_copy(q.at[:, head_columns(s)], qh.at[s], own_sem.at[2]),
    ]
    for copy in own:
        copy.start()
    pl.semaphore_wait(barrier, 6)

    def spread(i, a):
        to = lax.rem(s + i, 4)
        src = (k, v, q)[a].at[:, head_columns(to)]
        dst = qh.at[s] if a == 2 else kv.at[g_me, s, a]
        return pltpu.make_async_remote_copy(
            src_ref=src,
            dst_ref=dst,
            send_sem=s_send.at[i - 1, a],
            recv_sem=s_recv.at[i - 1, a],
            device_id=device(to, r, y),
            device_id_type=MESH,
        )

    sends = []
    for a in (0, 1):
        for i in (1, 3, 2):
            copy = spread(i, a)
            copy.start()
            sends.append(copy)

    def ring(t, j, rel, origin_r, origin_y, to_r, to_y):
        slot = kv.at[origin_r * 2 + origin_y, spread_from(ORDER[t]), j]
        return pltpu.make_async_remote_copy(
            src_ref=slot,
            dst_ref=slot,
            send_sem=g_send.at[t, j, rel],
            recv_sem=g_recv.at[t, j, rel],
            device_id=device(s, to_r, to_y),
            device_id_type=MESH,
        )

    def send(*args):
        copy = ring(*args)
        copy.start()
        sends.append(copy)

    def arrived(t, j, rel):
        ring(t, j, rel, r, y, right, y).wait_recv()

    for t in range(len(ORDER) + 2):
        if t < 4:
            for j in (0, 1):
                if ORDER[t] == 0:
                    own[j].wait()
                else:
                    spread(ORDER[t], j).wait_recv()
                send(t, j, 0, r, y, r, other)
                send(t, j, 1, r, y, right, y)
                send(t, j, 2, r, y, left, y)
        if t == 3:
            for i in (1, 3, 2):
                copy = spread(i, 2)
                copy.start()
                sends.append(copy)
        if 0 <= t - 1 < 4:
            for j in (0, 1):
                arrived(t - 1, j, 0)
                send(t - 1, j, 3, r, other, right, y)
                send(t - 1, j, 4, r, other, left, y)
            for j in (0, 1):
                arrived(t - 1, j, 1 + j)
                if j == 0:
                    send(t - 1, j, 5, left, y, right, y)
                else:
                    send(t - 1, j, 5, right, y, left, y)
        if 0 <= t - 2 < 4:
            for j in (0, 1):
                arrived(t - 2, j, 3 + j)
                if j == 0:
                    send(t - 2, j, 6, left, other, right, y)
                else:
                    send(t - 2, j, 6, right, other, left, y)
    for t in range(4):
        for j in (0, 1):
            for rel in (2 - j, 4 - j, 5, 6):
                arrived(t, j, rel)
    own[2].wait()
    for i in (1, 3, 2):
        spread(i, 2).wait_recv()
    for copy in sends:
        copy.wait_send()


def gather(q, k, v):
    rows = q.shape[0]
    anywhere = pl.BlockSpec(memory_space=pl.ANY)
    return pl.pallas_call(
        gather_kernel,
        name="spread_and_gather",
        out_shape=(
            jax.ShapeDtypeStruct((4, rows, HEAD), q.dtype),
            jax.ShapeDtypeStruct((8, 4, 2, rows, HEAD), q.dtype),
        ),
        in_specs=[anywhere] * 3,
        out_specs=(anywhere, anywhere),
        scratch_shapes=[
            pltpu.SemaphoreType.DMA((3,)),
            pltpu.SemaphoreType.DMA((3, 3)),
            pltpu.SemaphoreType.DMA((3, 3)),
            pltpu.SemaphoreType.DMA((4, 2, 7)),
            pltpu.SemaphoreType.DMA((4, 2, 7)),
        ],
        compiler_params=pltpu.CompilerParams(collective_id=0, has_side_effects=True),
    )(q, k, v)


def attend_kernel(lengths, layout, q, kv, out, logs, start, where_is, doc_at, top, total, summed):
    _, core, _, _, r, y = my_place()
    blocks, docs = layout.shape[0], lengths.shape[0]
    half = q.shape[1] // 2
    scale = 1.0 / math.sqrt(HEAD)

    def place(p, _):
        where_is[layout[p]] = p
        return 0

    lax.fori_loop(0, blocks, place, 0)

    def walk(j, at):
        start[j] = at
        end = at + lengths[j]

        def mark(b, _):
            doc_at[b] = j
            return 0

        lax.fori_loop(lax.div(at + half - 1, half), lax.div(end + half - 1, half), mark, 0)
        return end

    start[docs] = lax.fori_loop(0, docs, walk, 0)

    def one(u, _):
        s_q, h_q = lax.div(u, 2), lax.rem(u, 2)
        block = layout[ctx_of(core, s_q, r, y) * 2 + h_q]
        base = block * half
        first_doc = doc_at[block]
        rows = pl.ds(pl.multiple_of(h_q * half, half), half)
        query = q[s_q, rows, :]
        q_pos = base + lax.broadcasted_iota(jnp.int32, (1, half), 1)

        def doc_start(state):
            j, low = state
            at = start[j]
            return j + 1, jnp.where(q_pos >= at, at, low)

        _, low = lax.while_loop(
            lambda state: start[state[0]] < base + half,
            doc_start,
            (first_doc + 1, jnp.full((1, half), start[first_doc], jnp.int32)),
        )
        first_block = lax.div(start[first_doc], half)
        top[...] = jnp.full(top.shape, -1e30, jnp.float32)
        total[...] = jnp.zeros(total.shape, jnp.float32)
        summed[...] = jnp.zeros(summed.shape, jnp.float32)

        def step(n, _):
            key_block = block - n
            p = where_is[key_block]
            d, h_k = lax.div(p, 2), lax.rem(p, 2)
            z, x, y_k = lax.div(d, 8), lax.rem(lax.div(d, 2), 4), lax.rem(d, 2)
            s_k = z * (1 - core) + x * core
            r_k = x * (1 - core) + z * core
            key_rows = pl.ds(pl.multiple_of(h_k * half, half), half)
            key = kv[r_k * 2 + y_k, s_k, 0, key_rows, :]
            value = kv[r_k * 2 + y_k, s_k, 1, key_rows, :]
            scores = lax.dot_general(
                key, query, (((1,), (1,)), ((), ())), preferred_element_type=jnp.float32
            )
            k_pos = key_block * half + lax.broadcasted_iota(jnp.int32, (half, half), 0)
            scores = jnp.where((k_pos >= low) & (k_pos <= q_pos), scores, -1e30)
            old = top[...]
            new = jnp.maximum(old, jnp.max(scores, axis=0, keepdims=True))
            weights = jnp.exp2((scores - new) * (scale * LOG2E))
            factor = jnp.exp2((old - new) * (scale * LOG2E))
            top[...] = new
            total[...] = total[...] * factor + jnp.sum(weights, axis=0, keepdims=True)
            summed[...] = summed[...] * factor + lax.dot_general(
                value,
                weights.astype(jnp.bfloat16),
                (((0,), (0,)), ((), ())),
                preferred_element_type=jnp.float32,
            )
            return 0

        lax.fori_loop(0, block - first_block + 1, step, 0)
        out[s_q, rows, :] = (summed[...] / total[...]).T.astype(out.dtype)
        logs[s_q, :, rows] = top[...] * scale + jnp.log(total[...])
        return 0

    lax.fori_loop(0, 8, one, 0)


def attend(lengths, layout, q, kv):
    rows = q.shape[1]
    small, near = pl.BlockSpec(memory_space=pltpu.SMEM), pl.BlockSpec(memory_space=pltpu.VMEM)
    return pl.pallas_call(
        attend_kernel,
        name="attend",
        out_shape=(
            jax.ShapeDtypeStruct((4, rows, HEAD), q.dtype),
            jax.ShapeDtypeStruct((4, 1, rows), jnp.float32),
        ),
        in_specs=[small, small, near, near],
        out_specs=(near, near),
        scratch_shapes=[
            pltpu.SMEM((lengths.shape[0] + 1,), jnp.int32),
            pltpu.SMEM((layout.shape[0],), jnp.int32),
            pltpu.SMEM((layout.shape[0],), jnp.int32),
            pltpu.VMEM((1, rows // 2), jnp.float32),
            pltpu.VMEM((1, rows // 2), jnp.float32),
            pltpu.VMEM((HEAD, rows // 2), jnp.float32),
        ],
        compiler_params=pltpu.CompilerParams(vmem_limit_bytes=40 * 1024 * 1024),
    )(lengths, layout, q, kv)


CHUNKS = 4


def project_kernel(
    o, logs, w, mixed, log_out,
    w_near, att, logs_in, own_sum, c_out, c_in, y_out, y_in,
    w_sem, own_sem, a_send, a_recv, l_send, l_recv, c_send, c_recv, y_send, y_recv,
):
    tp, core, high, s, r, y = my_place()
    me = lax.axis_index("ctx")
    rows, columns = mixed.shape
    part = rows // CHUNKS
    targets = ((1 - high) * 2 + 1 - core, (1 - high) * 2 + core, high * 2 + 1 - core, tp)
    loads = []
    for n, target in enumerate(targets):
        at = pl.ds(pl.multiple_of(target * columns, columns), columns)
        copy = pltpu.make_async_copy(w.at[:, at], w_near.at[n], w_sem.at[n])
        copy.start()
        loads.append(copy)
    mate, across = (me, targets[2]), (me, targets[1])
    barrier = pltpu.get_barrier_semaphore()
    partners = [(ctx_of(core, lax.rem(s + i, 4), r, y), tp) for i in (1, 2, 3)] + [mate, across]
    for partner in partners:
        pl.semaphore_signal(barrier, inc=1, device_id=partner, device_id_type=MESH)
    own = [
        pltpu.make_async_copy(o.at[s], att.at[:, head_columns(s)], own_sem.at[0]),
        pltpu.make_async_copy(logs.at[s], logs_in.at[s], own_sem.at[1]),
    ]
    for copy in own:
        copy.start()
    pl.semaphore_wait(barrier, 5)

    sends = []

    def remote(src, dst, send_sem, recv_sem, to):
        return pltpu.make_async_remote_copy(
            src_ref=src, dst_ref=dst, send_sem=send_sem, recv_sem=recv_sem,
            device_id=to, device_id_type=MESH,
        )

    back, back_logs = [], []
    for i in (2, 1, 3):
        to = lax.rem(s + i, 4)
        device = (ctx_of(core, to, r, y), tp)
        back.append(
            remote(o.at[to], att.at[:, head_columns(s)], a_send.at[i - 1], a_recv.at[i - 1], device)
        )
        back_logs.append(
            remote(logs.at[to], logs_in.at[s], l_send.at[i - 1], l_recv.at[i - 1], device)
        )
    for copy in back + back_logs:
        copy.start()
        sends.append(copy)
    own[0].wait()
    for copy in back:
        copy.wait_recv()

    def chunk(c):
        return pl.ds(c * part, part)

    def product(c, n):
        return jnp.dot(att[chunk(c), :], w_near[n], preferred_element_type=jnp.float32)

    def to_mate(c, m):
        return remote(
            c_out.at[m, chunk(c)], c_in.at[m, chunk(c)], c_send.at[m, c], c_recv.at[m, c], mate
        )

    def to_across(c):
        return remote(y_out.at[chunk(c)], y_in.at[chunk(c)], y_send.at[c], y_recv.at[c], across)

    loads[0].wait()
    for c in range(CHUNKS):
        c_out[0, chunk(c), :] = product(c, 0).astype(jnp.bfloat16)
        copy = to_mate(c, 0)
        copy.start()
        sends.append(copy)
    loads[1].wait()
    for c in range(CHUNKS):
        mine = product(c, 1)
        to_mate(c, 0).wait_recv()
        y_out[chunk(c), :] = (mine + c_in[0, chunk(c), :].astype(jnp.float32)).astype(jnp.bfloat16)
        copy = to_across(c)
        copy.start()
        sends.append(copy)
    loads[2].wait()
    for c in range(CHUNKS):
        c_out[1, chunk(c), :] = product(c, 2).astype(jnp.bfloat16)
        copy = to_mate(c, 1)
        copy.start()
        sends.append(copy)
    loads[3].wait()
    for c in range(CHUNKS):
        mine = product(c, 3)
        to_mate(c, 1).wait_recv()
        own_sum[chunk(c), :] = mine + c_in[1, chunk(c), :].astype(jnp.float32)
    own[1].wait()
    for copy in back_logs:
        copy.wait_recv()
    for h in range(4):
        log_out[h : h + 1, :] = logs_in[h]
    for c in range(CHUNKS):
        to_across(c).wait_recv()
        mixed[chunk(c), :] = (own_sum[chunk(c), :] + y_in[chunk(c), :].astype(jnp.float32)).astype(
            jnp.bfloat16
        )
    for copy in sends:
        copy.wait_send()


def project(o, logs, w):
    rows, depth, columns = o.shape[1], w.shape[0], w.shape[1] // 4
    anywhere, near = pl.BlockSpec(memory_space=pl.ANY), pl.BlockSpec(memory_space=pltpu.VMEM)
    dma = pltpu.SemaphoreType.DMA
    return pl.pallas_call(
        project_kernel,
        name="return_and_project",
        out_shape=(
            jax.ShapeDtypeStruct((rows, columns), jnp.bfloat16),
            jax.ShapeDtypeStruct((4, rows), jnp.float32),
        ),
        in_specs=[anywhere, anywhere, anywhere],
        out_specs=(near, near),
        scratch_shapes=[
            pltpu.VMEM((4, depth, columns), jnp.bfloat16),
            pltpu.VMEM((rows, depth), jnp.bfloat16),
            pltpu.VMEM((4, 1, rows), jnp.float32),
            pltpu.VMEM((rows, columns), jnp.float32),
            pltpu.VMEM((2, rows, columns), jnp.bfloat16),
            pltpu.VMEM((2, rows, columns), jnp.bfloat16),
            pltpu.VMEM((rows, columns), jnp.bfloat16),
            pltpu.VMEM((rows, columns), jnp.bfloat16),
            dma((4,)), dma((2,)), dma((3,)), dma((3,)), dma((3,)), dma((3,)),
            dma((2, CHUNKS)), dma((2, CHUNKS)), dma((CHUNKS,)), dma((CHUNKS,)),
        ],
        compiler_params=pltpu.CompilerParams(
            collective_id=1, has_side_effects=True, vmem_limit_bytes=40 * 1024 * 1024
        ),
    )(o, logs, w)


def local(queries, keys, values, out_weight, doc_lengths, layout):
    qh, kv = gather(queries, keys, values)
    o, logs = attend(doc_lengths, layout, qh, kv)
    return project(o, logs, out_weight)


def solution(mesh):
    placed = (P("ctx", "tp"), P("ctx", "tp"), P("ctx", "tp"), P("tp", None), P(), P())
    return jax.shard_map(
        local,
        mesh=mesh,
        in_specs=placed,
        out_specs=(P("ctx", "tp"), P("tp", "ctx")),
        check_vma=False,
    )
```

time: 843 us -> 118 us (0.14)
  the two profiles are of different devices: /device:TPU:32 before, /device:TPU:1 now
where the time goes in v1:
time: 118 us
  Pallas kernels  110 us (93%)
  local copies, waits for them, and re-layouts  7.3 us (6%)
    pallas_call x1, Pallas kernels, gather(): pl.pallas_call(gather_kernel, name='spread_and_gather', out_shape=(jax.Sh...  53 us
    pallas_call x1, Pallas kernels, project(): pl.pallas_call(project_kernel, name='return_and_project', out_shape=(jax....  41.7 us
    pallas_call x1, Pallas kernels, attend(): pl.pallas_call(attend_kernel, name='attend', out_shape=(jax.ShapeDtypeStr...  15 us
    unnamed x12, local copies, waits for them, and re-layouts  7.3 us

profile of v1, /device:TPU:1, one launch (start us, length us, event | category | flops | bytes accessed | tf_op | source)
XLA Modules:
  0.0 117.7 jit_solution(5932643441709302424)
XLA Ops:
  0.6 53.0 %spread_and_gather.1 = (bf16[4,512,128]{2,1,0:T(8,128)(2,1)}, bf16[8,4,2,512,128]{4,3,2,1,0:T(8,128)(2,1)}) custom-call(bf16[512,512]{1,0:T(8,128)(2,1)} %q.1, bf16[512,512]{1,0:T(8,128)(2,1)} %k.1, bf16[512,512]{1,0:T(8,128)(2,1)} %v.1), custom_call_target="tpu_custom_call" | custom-call | tf_op jit(solution)/shard_map/spread_and_gather/pallas_call | solution.py:145
  53.7 0.0 copy-start
  53.7 3.4 %copy-done = bf16[8,4,2,512,128]{4,3,2,1,0:T(8,128)(2,1)S(1)} copy-done((bf16[8,4,2,512,128]{4,3,2,1,0:T(8,128)(2,1)S(1)}, bf16[8,4,2,512,128]{4,3,2,1,0:T(8,128)(2,1)}, u32[]{:S(2)}) %copy-start) | copy-done | bytes 8388632
  57.1 0.0 copy-start.2
  57.1 1.0 copy-done.2
  58.1 0.0 copy-start.3
  58.1 0.7 copy-done.3
  58.8 0.0 copy-start.4
  58.8 0.7 copy-done.4
  59.4 0.0 copy-start.1
  59.4 15.0 %attend.1 = (bf16[4,512,128]{2,1,0:T(8,128)(2,1)S(1)}, f32[4,1,512]{2,1,0:T(1,128)S(1)}) custom-call(s32[64]{0:T(128)S(1)} %copy-done.3, s32[64]{0:T(128)S(1)} %copy-done.4, bf16[4,512,128]{2,1,0:T(8,128)(2,1)S(1)} %copy-done.2, bf16[8,4,2,512,128]{4,3,2,1,0:T(8,128)(2,1)S(1)} %copy-done), custom_call_target="tpu_custom_call" | custom-call | tf_op jit(solution)/shard_map/attend/pallas_call | solution.py:254
  74.5 0.0 copy-done.1
  74.5 41.7 %return_and_project.1 = (bf16[512,1024]{1,0:T(8,128)(2,1)S(1)}, f32[4,512]{1,0:T(4,128)S(1)}) custom-call(bf16[4,512,128]{2,1,0:T(8,128)(2,1)S(1)} %get-tuple-element.8.o, f32[4,1,512]{2,1,0:T(1,128)S(1)} %get-tuple-element.9.logs, bf16[512,4096]{1,0:T(8,128)(2,1)S(1)} %copy-done.1), custom_call_target="tpu_custom_call" | custom-call | tf_op jit(solution)/shard_map/return_and_project/pallas_call | solution.py:389
  116.2 1.0 copy.10
  117.1 0.6 copy.11
Async XLA Ops:
  53.7 3.4 %copy-start = (bf16[8,4,2,512,128]{4,3,2,1,0:T(8,128)(2,1)S(1)}, bf16[8,4,2,512,128]{4,3,2,1,0:T(8,128)(2,1)}, u32[]{:S(2)}) copy-start(bf16[8,4,2,512,128]{4,3,2,1,0:T(8,128)(2,1)} %get-tuple-element.7.kv) | copy-start | bytes 25165828
  57.1 1.0 copy-start.2
  58.1 0.7 copy-start.3
  58.8 0.7 copy-start.4
  59.4 15.0 %copy-start.1 = (bf16[512,4096]{1,0:T(8,128)(2,1)S(1)}, bf16[512,4096]{1,0:T(8,128)(2,1)}, u32[]{:S(2)}) copy-start(bf16[512,4096]{1,0:T(8,128)(2,1)} %w.1) | copy-start | bytes 12582916

commit v2 on v1

v2 whole, which is shorter than its diff:
```python
import math

import jax
import jax.numpy as jnp
from jax import lax
from jax.experimental import pallas as pl
from jax.experimental.pallas import tpu as pltpu
from jax.sharding import PartitionSpec as P

HEAD = 128
MESH = pl.DeviceIdType.MESH
SCALE = 1.0 / math.sqrt(HEAD)
LOG2E = math.log2(math.e)
STREAMS = 4
LEAST = -1e29
VMEM_BYTES = 40 * 1024 * 1024


def ctx_of(core, p, r, y):
    return p * (8 - 6 * core) + r * (2 + 6 * core) + y


def split_ctx(ctx, core):
    z, x, y = lax.div(ctx, 8), lax.rem(lax.div(ctx, 2), 4), lax.rem(ctx, 2)
    return z * (1 - core) + x * core, x * (1 - core) + z * core, y


def pair_bit(p):
    return lax.rem(lax.div(p + 1, 2), 2)


def member_place(pair, m):
    bit = lax.rem(m, 2)
    return bit + pair * (3 - 2 * bit), lax.div(m, 2)


class Place:
    def __init__(self):
        self.ctx, self.tp = lax.axis_index("ctx"), lax.axis_index("tp")
        self.core, self.high = lax.rem(self.tp, 2), lax.div(self.tp, 2)
        self.p, self.r, self.y = split_ctx(self.ctx, self.core)
        self.pair, self.bit = lax.div(self.p, 2), pair_bit(self.p)
        self.m = self.y * 2 + self.bit

    def member(self, i):
        bit = 1 - self.bit if i % 2 else self.bit
        y = 1 - self.y if i // 2 else self.y
        return y * 2 + bit

    def at_member(self, m):
        p, y = member_place(self.pair, m)
        return (ctx_of(self.core, p, self.r, y), self.tp)

    def at_ring(self, r):
        return (ctx_of(self.core, self.p, r, self.y), self.tp)

    def at_twin(self):
        return (ctx_of(self.core, 3 - self.p, self.r, self.y), self.tp)


def head_columns(m):
    return pl.ds(pl.multiple_of(m * HEAD, HEAD), HEAD)


def remote(src, dst, send_sem, recv_sem, to):
    return pltpu.make_async_remote_copy(
        src_ref=src, dst_ref=dst, send_sem=send_sem, recv_sem=recv_sem,
        device_id=to, device_id_type=MESH,
    )


def greet(partners):
    barrier = pltpu.get_barrier_semaphore()
    for partner in partners:
        pl.semaphore_signal(barrier, inc=1, device_id=partner, device_id_type=MESH)
    return lambda: pl.semaphore_wait(barrier, len(partners))


def gather_kernel(q, k, v, qh, kv, own_sem, s_send, s_recv, g_send, g_recv, t_send, t_recv):
    me = Place()
    left, right = lax.rem(me.r + 3, 4), lax.rem(me.r + 1, 4)
    wait_all = greet(
        [me.at_member(me.member(i)) for i in (1, 2, 3)]
        + [me.at_ring(left), me.at_ring(right), me.at_twin()]
    )
    mine = head_columns(me.m)
    own = [
        pltpu.make_async_copy(k.at[:, mine], kv.at[me.r, me.m, 0], own_sem.at[0]),
        pltpu.make_async_copy(v.at[:, mine], kv.at[me.r, me.m, 1], own_sem.at[1]),
        pltpu.make_async_copy(q.at[:, mine], qh.at[me.pair, me.m], own_sem.at[2]),
    ]
    for copy in own:
        copy.start()
    wait_all()

    sends = []

    def start(copy):
        copy.start()
        sends.append(copy)

    def spread(i, a):
        to = me.member(i)
        dst = qh.at[me.pair, me.m] if a == 2 else kv.at[me.r, me.m, a]
        return remote(
            (k, v, q)[a].at[:, head_columns(to)], dst,
            s_send.at[i - 1, a], s_recv.at[i - 1, a], me.at_member(to),
        )

    def ring(i, j, rel, origin, to):
        slot = kv.at[origin, me.member(i), j]
        return remote(slot, slot, g_send.at[i, j, rel], g_recv.at[i, j, rel], me.at_ring(to))

    def twin(i):
        slot = qh.at[me.pair, me.member(i)]
        return remote(slot, slot, t_send.at[i], t_recv.at[i], me.at_twin())

    def arrived(i, j, rel):
        ring(i, j, rel, me.r, right).wait_recv()

    for a in (0, 1, 2):
        for i in (1, 2, 3):
            start(spread(i, a))
    for i in range(5):
        if i < 4:
            for j in (0, 1):
                if i == 0:
                    own[j].wait()
                else:
                    spread(i, j).wait_recv()
                start(ring(i, j, 0, me.r, right))
                start(ring(i, j, 1, me.r, left))
        if i >= 1:
            arrived(i - 1, 0, 0)
            start(ring(i - 1, 0, 2, left, right))
            arrived(i - 1, 1, 1)
            start(ring(i - 1, 1, 2, right, left))
    own[2].wait()
    start(twin(0))
    for i in (1, 2, 3):
        spread(i, 2).wait_recv()
        start(twin(i))
    for i in range(4):
        arrived(i, 0, 1)
        arrived(i, 1, 0)
        arrived(i, 0, 2)
        arrived(i, 1, 2)
        twin(i).wait_recv()
    for copy in sends:
        copy.wait_send()


def gather(q, k, v):
    rows = q.shape[0]
    anywhere, near = pl.BlockSpec(memory_space=pltpu.HBM), pl.BlockSpec(memory_space=pltpu.VMEM)
    dma = pltpu.SemaphoreType.DMA
    return pl.pallas_call(
        gather_kernel,
        name="spread_and_gather",
        out_shape=(
            jax.ShapeDtypeStruct((2, 4, rows, HEAD), q.dtype),
            jax.ShapeDtypeStruct((4, 4, 2, rows, HEAD), q.dtype),
        ),
        in_specs=[anywhere] * 3,
        out_specs=(near, near),
        scratch_shapes=[
            dma((3,)), dma((3, 3)), dma((3, 3)), dma((4, 2, 3)), dma((4, 2, 3)), dma((4,)), dma((4,)),
        ],
        compiler_params=pltpu.CompilerParams(
            collective_id=0, has_side_effects=True, vmem_limit_bytes=VMEM_BYTES
        ),
    )(q, k, v)


def attend_kernel(
    far_lengths, far_layout, q, kv, out, logs,
    lengths, layout, start, where_is, doc_at, work, count, lows, top, total, summed, table_sem,
):
    me = Place()
    tables = [
        pltpu.make_async_copy(far_lengths, lengths, table_sem.at[0]),
        pltpu.make_async_copy(far_layout, layout, table_sem.at[1]),
    ]
    for copy in tables:
        copy.start()
    top[...] = jnp.full(top.shape, LEAST, jnp.float32)
    total[...] = jnp.zeros(total.shape, jnp.float32)
    for copy in tables:
        copy.wait()
    blocks, docs = layout.shape[0], lengths.shape[0]
    half = q.shape[2] // 2
    spare = 16

    def place(b, _):
        where_is[layout[b]] = b
        return 0

    lax.fori_loop(0, blocks, place, 0)

    def walk(j, at):
        start[j] = at
        end = at + lengths[j]

        def mark(b, _):
            doc_at[b] = j
            return 0

        lax.fori_loop(lax.div(at + half - 1, half), lax.div(end + half - 1, half), mark, 0)
        return end

    start[docs] = lax.fori_loop(0, docs, walk, 0)
    for n in range(STREAMS):
        count[n] = 0

    def query_block(u):
        p, y = member_place(lax.div(u, 8), lax.rem(lax.div(u, 2), 4))
        return layout[ctx_of(me.core, p, me.r, y) * 2 + lax.rem(u, 2)]

    def plan(u, _):
        block = query_block(u)
        base = block * half
        first_doc = doc_at[block]
        q_pos = base + lax.broadcasted_iota(jnp.int32, (1, half), 1)

        def doc_start(state):
            j, low = state
            at = start[j]
            return j + 1, jnp.where(q_pos >= at, at, low)

        _, low = lax.while_loop(
            lambda state: start[state[0]] < base + half,
            doc_start,
            (first_doc + 1, jnp.full((1, half), start[first_doc], jnp.int32)),
        )
        lows[u] = low
        summed[u] = jnp.zeros((HEAD, half), jnp.float32)
        stream = jnp.int32(0)
        for n in range(1, STREAMS):
            stream = jnp.where(count[n] < count[stream], n, stream)

        def add(key_block, filled):
            at = where_is[key_block]
            p, r, y = split_ctx(lax.div(at, 2), me.core)
            slot = r * 8 + (y * 2 + pair_bit(p)) * 2 + lax.rem(at, 2)
            work[stream, filled] = (u * blocks + key_block) * 32 + slot
            return filled + jnp.where(lax.div(p, 2) == me.pair, 1, 0)

        count[stream] = lax.fori_loop(
            lax.div(start[first_doc], half), block + 1, add, count[stream]
        )
        return 0

    lax.fori_loop(0, 16, plan, 0)
    steps = count[0]
    for n in range(1, STREAMS):
        steps = jnp.maximum(steps, count[n])
    for n in range(STREAMS):

        def fill(t, _):
            work[n, t] = (spare + n) * blocks * 32
            return 0

        lax.fori_loop(count[n], steps, fill, 0)

    def step(t, _):
        todo = []
        for n in range(STREAMS):
            code = work[n, t]
            slot = lax.rem(code, 32)
            key_block = lax.rem(lax.div(code, 32), blocks)
            u = lax.div(code, 32 * blocks)
            real = jnp.minimum(u, spare - 1)
            q_rows = pl.ds(pl.multiple_of(lax.rem(real, 2) * half, half), half)
            k_rows = pl.ds(pl.multiple_of(lax.rem(slot, 2) * half, half), half)
            r_k, m_k = lax.div(slot, 8), lax.rem(lax.div(slot, 2), 4)
            query = q[lax.div(real, 8), lax.rem(lax.div(real, 2), 4), q_rows, :]
            key, value = kv[r_k, m_k, 0, k_rows, :], kv[r_k, m_k, 1, k_rows, :]
            q_pos = query_block(real) * half + lax.broadcasted_iota(jnp.int32, (1, half), 1)
            todo.append((u, key_block, query, key, value, q_pos, lows[real]))
        scores = [
            lax.dot_general(key, query, (((1,), (1,)), ((), ())), preferred_element_type=jnp.float32)
            for _, _, query, key, _, _, _ in todo
        ]
        for n, (u, key_block, _, _, value, q_pos, low) in enumerate(todo):
            k_pos = key_block * half + lax.broadcasted_iota(jnp.int32, (half, half), 0)
            masked = jnp.where((k_pos >= low) & (k_pos <= q_pos), scores[n], -1e30)
            old = top[u]
            new = jnp.maximum(old, jnp.max(masked, axis=0, keepdims=True))
            weights = jnp.exp2((masked - new) * (SCALE * LOG2E))
            factor = jnp.exp2((old - new) * (SCALE * LOG2E))
            top[u] = new
            total[u] = total[u] * factor + jnp.sum(weights, axis=0, keepdims=True)
            summed[u] = summed[u] * factor + lax.dot_general(
                value,
                weights.astype(jnp.bfloat16),
                (((0,), (0,)), ((), ())),
                preferred_element_type=jnp.float32,
            )
        return 0

    lax.fori_loop(0, steps, step, 0)

    def finish(u, _):
        at = (lax.div(u, 8), lax.rem(lax.div(u, 2), 4))
        rows = pl.ds(pl.multiple_of(lax.rem(u, 2) * half, half), half)
        some = total[u] > 0.0
        safe = jnp.where(some, total[u], 1.0)
        out[at[0], at[1], :, rows] = (summed[u] * (1.0 / safe)).astype(out.dtype)
        logs[at[0], at[1], :, rows] = jnp.where(some, top[u] * SCALE + jnp.log(safe), -1e30)
        return 0

    lax.fori_loop(0, 16, finish, 0)


def attend(lengths, layout, q, kv):
    rows, blocks = q.shape[2], layout.shape[0]
    half = rows // 2
    far, near = pl.BlockSpec(memory_space=pltpu.HBM), pl.BlockSpec(memory_space=pltpu.VMEM)
    return pl.pallas_call(
        attend_kernel,
        name="attend",
        out_shape=(
            jax.ShapeDtypeStruct((2, 4, HEAD, rows), q.dtype),
            jax.ShapeDtypeStruct((2, 4, 1, rows), jnp.float32),
        ),
        in_specs=[far, far, near, near],
        out_specs=(near, near),
        scratch_shapes=[
            pltpu.SMEM(lengths.shape, jnp.int32),
            pltpu.SMEM(layout.shape, jnp.int32),
            pltpu.SMEM((lengths.shape[0] + 1,), jnp.int32),
            pltpu.SMEM((blocks,), jnp.int32),
            pltpu.SMEM((blocks,), jnp.int32),
            pltpu.SMEM((STREAMS, 16 * blocks + 1), jnp.int32),
            pltpu.SMEM((STREAMS,), jnp.int32),
            pltpu.VMEM((16, 1, half), jnp.int32),
            pltpu.VMEM((16 + STREAMS, 1, half), jnp.float32),
            pltpu.VMEM((16 + STREAMS, 1, half), jnp.float32),
            pltpu.VMEM((16 + STREAMS, HEAD, half), jnp.float32),
            pltpu.SemaphoreType.DMA((2,)),
        ],
        compiler_params=pltpu.CompilerParams(vmem_limit_bytes=VMEM_BYTES),
    )(lengths, layout, q, kv)


CHUNKS = 4


def project_kernel(
    o, logs, w, mixed, log_out,
    o_in, lo_in, merged, merged_logs, att, logs_in, own_sum, c_out, c_in, y_out, y_in,
    b_send, b_recv, lb_sem, a_send, a_recv, l_send, l_recv, c_send, c_recv, y_send, y_recv,
):
    me = Place()
    rows, columns = mixed.shape
    part = rows // CHUNKS
    high, core = me.high, me.core
    targets = ((1 - high) * 2 + 1 - core, (1 - high) * 2 + core, high * 2 + 1 - core, me.tp)
    mate, across = (me.ctx, targets[2]), (me.ctx, targets[1])
    greet(
        [me.at_member(me.member(i)) for i in (1, 2, 3)] + [me.at_twin(), mate, across]
    )()
    sends = []

    def start(copy):
        copy.start()
        sends.append(copy)

    order = (3, 1, 2, 0)

    def to_twin(i):
        m = me.member(i)
        return remote(o.at[1 - me.pair, m], o_in.at[m], b_send.at[i], b_recv.at[i], me.at_twin())

    def to_owner(i):
        m = me.member(i)
        return remote(
            merged.at[i - 1], att.at[:, head_columns(me.m)],
            a_send.at[i - 1], a_recv.at[i - 1], me.at_member(m),
        )

    def log_to_owner(i):
        m = me.member(i)
        return remote(
            merged_logs.at[i - 1], logs_in.at[me.m],
            l_send.at[i - 1], l_recv.at[i - 1], me.at_member(m),
        )

    twin_logs = remote(logs.at[1 - me.pair], lo_in, lb_sem.at[0], lb_sem.at[1], me.at_twin())
    start(twin_logs)
    for i in order:
        start(to_twin(i))
    twin_logs.wait_recv()
    for i in order:
        m = me.member(i)
        one, two = logs[me.pair, m], lo_in[m]
        most = jnp.maximum(one, two)
        e_one, e_two = jnp.exp(one - most), jnp.exp(two - most)
        both = e_one + e_two
        final = most + jnp.log(both)
        share = 1.0 / both
        to_twin(i).wait_recv()
        whole = o[me.pair, m].astype(jnp.float32) * (e_one * share) + o_in[m].astype(
            jnp.float32
        ) * (e_two * share)
        turned = whole.T.astype(jnp.bfloat16)
        if i == 0:
            att[:, head_columns(me.m)] = turned
            logs_in[me.m] = final
        else:
            merged[i - 1] = turned
            merged_logs[i - 1] = final
            start(to_owner(i))
            start(log_to_owner(i))
    for i in (1, 2, 3):
        to_owner(i).wait_recv()

    def chunk(c):
        return pl.ds(c * part, part)

    def product(c, n):
        at = pl.ds(pl.multiple_of(targets[n] * columns, columns), columns)
        return jnp.dot(att[chunk(c), :], w[:, at], preferred_element_type=jnp.float32)

    def to_mate(c, n):
        return remote(
            c_out.at[n, chunk(c)], c_in.at[n, chunk(c)], c_send.at[n, c], c_recv.at[n, c], mate
        )

    def to_across(c):
        return remote(y_out.at[chunk(c)], y_in.at[chunk(c)], y_send.at[c], y_recv.at[c], across)

    def give(c, n):
        c_out[n, chunk(c), :] = product(c, 2 * n).astype(jnp.bfloat16)
        start(to_mate(c, n))

    def pass_on(c):
        mine = product(c, 1)
        to_mate(c, 0).wait_recv()
        y_out[chunk(c), :] = (mine + c_in[0, chunk(c), :].astype(jnp.float32)).astype(jnp.bfloat16)
        start(to_across(c))

    give(0, 0)
    for c in range(CHUNKS):
        if c + 1 < CHUNKS:
            give(c + 1, 0)
        pass_on(c)
    for c in range(CHUNKS):
        give(c, 1)
    for c in range(CHUNKS):
        mine = product(c, 3)
        to_mate(c, 1).wait_recv()
        own_sum[chunk(c), :] = mine + c_in[1, chunk(c), :].astype(jnp.float32)
    for i in (1, 2, 3):
        log_to_owner(i).wait_recv()
    for h in range(4):
        log_out[h : h + 1, :] = logs_in[h]
    for c in range(CHUNKS):
        to_across(c).wait_recv()
        mixed[chunk(c), :] = (own_sum[chunk(c), :] + y_in[chunk(c), :].astype(jnp.float32)).astype(
            jnp.bfloat16
        )
    for copy in sends:
        copy.wait_send()


def project(o, logs, w):
    rows, depth, columns = o.shape[3], w.shape[0], w.shape[1] // 4
    near = pl.BlockSpec(memory_space=pltpu.VMEM)
    dma = pltpu.SemaphoreType.DMA
    return pl.pallas_call(
        project_kernel,
        name="return_and_project",
        out_shape=(
            jax.ShapeDtypeStruct((rows, columns), jnp.bfloat16),
            jax.ShapeDtypeStruct((4, rows), jnp.float32),
        ),
        in_specs=[near, near, near],
        out_specs=(near, near),
        scratch_shapes=[
            pltpu.VMEM((4, HEAD, rows), jnp.bfloat16),
            pltpu.VMEM((4, 1, rows), jnp.float32),
            pltpu.VMEM((3, rows, HEAD), jnp.bfloat16),
            pltpu.VMEM((3, 1, rows), jnp.float32),
            pltpu.VMEM((rows, depth), jnp.bfloat16),
            pltpu.VMEM((4, 1, rows), jnp.float32),
            pltpu.VMEM((rows, columns), jnp.float32),
            pltpu.VMEM((2, rows, columns), jnp.bfloat16),
            pltpu.VMEM((2, rows, columns), jnp.bfloat16),
            pltpu.VMEM((rows, columns), jnp.bfloat16),
            pltpu.VMEM((rows, columns), jnp.bfloat16),
            dma((4,)), dma((4,)), dma((2,)), dma((3,)), dma((3,)), dma((3,)), dma((3,)),
            dma((2, CHUNKS)), dma((2, CHUNKS)), dma((CHUNKS,)), dma((CHUNKS,)),
        ],
        compiler_params=pltpu.CompilerParams(
            collective_id=1, has_side_effects=True, vmem_limit_bytes=VMEM_BYTES
        ),
    )(o, logs, w)


def local(queries, keys, values, out_weight, doc_lengths, layout):
    qh, kv = gather(queries, keys, values)
    o, logs = attend(doc_lengths, layout, qh, kv)
    return project(o, logs, out_weight)


def solution(mesh):
    placed = (P("ctx", "tp"), P("ctx", "tp"), P("ctx", "tp"), P("tp", None), P(), P())
    return jax.shard_map(
        local,
        mesh=mesh,
        in_specs=placed,
        out_specs=(P("ctx", "tp"), P("tp", "ctx")),
        check_vma=False,
    )
```

time: 118 us -> 100 us (0.85)
  Pallas kernels: 110 us -> 92.9 us
    pallas_call x1, Pallas kernels: 53 us -> 39 us  [gather(): pl.pallas_call(gather_kernel, name='spread_and_gather', out_shape=(jax.Sh...]
    pallas_call x1, Pallas kernels: 15 us -> 10.5 us  [attend(): pl.pallas_call(attend_kernel, name='attend', out_shape=(jax.ShapeDtypeStr...]
    pallas_call x1, Pallas kernels: 41.7 us -> 43.3 us  [project(): pl.pallas_call(project_kernel, name='return_and_project', out_shape=(jax....]
    unnamed x12 -> x14, local copies, waits for them, and re-layouts: 7.3 us -> 6.36 us
where the time goes in v2:
time: 100 us; the launch traced here: 99.9 us
  Pallas kernels  92.9 us (93%)
  local copies, waits for them, and re-layouts  6.36 us (6%)
    pallas_call x1, Pallas kernels, project(): pl.pallas_call(project_kernel, name='return_and_project', out_shape=(jax....  43.3 us
    pallas_call x1, Pallas kernels, gather(): pl.pallas_call(gather_kernel, name='spread_and_gather', out_shape=(jax.Sh...  39 us
    pallas_call x1, Pallas kernels, attend(): pl.pallas_call(attend_kernel, name='attend', out_shape=(jax.ShapeDtypeStr...  10.5 us
    unnamed x14, local copies, waits for them, and re-layouts  6.36 us

profile of v2, /device:TPU:1, one launch (start us, length us, event | category | flops | bytes accessed | tf_op | source)
XLA Modules:
  0.0 99.9 jit_solution(1584943326190208481)
XLA Ops:
  0.6 0.0 copy-start
  0.6 0.0 copy-start.1
  0.7 1.2 %copy-done.1 = bf16[512,512]{1,0:T(8,128)(2,1)S(1)} copy-done((bf16[512,512]{1,0:T(8,128)(2,1)S(1)}, bf16[512,512]{1,0:T(8,128)(2,1)}, u32[]{:S(2)}) %copy-start.1) | copy-done | bytes 524312
  1.8 0.0 copy-start.2
  1.8 1.3 %copy-done.2 = bf16[512,512]{1,0:T(8,128)(2,1)S(1)} copy-done((bf16[512,512]{1,0:T(8,128)(2,1)S(1)}, bf16[512,512]{1,0:T(8,128)(2,1)}, u32[]{:S(2)}) %copy-start.2) | copy-done | bytes 524312
  3.1 0.0 copy-start.3
  3.1 1.0 %copy-done.3 = bf16[512,512]{1,0:T(8,128)(2,1)S(1)} copy-done((bf16[512,512]{1,0:T(8,128)(2,1)S(1)}, bf16[512,512]{1,0:T(8,128)(2,1)}, u32[]{:S(2)}) %copy-start.3) | copy-done | bytes 524312
  4.1 39.0 %spread_and_gather.1 = (bf16[2,4,512,128]{3,2,1,0:T(8,128)(2,1)S(1)}, bf16[4,4,2,512,128]{4,3,2,1,0:T(8,128)(2,1)S(1)}) custom-call(bf16[512,512]{1,0:T(8,128)(2,1)S(1)} %copy-done.1, bf16[512,512]{1,0:T(8,128)(2,1)S(1)} %copy-done.2, bf16[512,512]{1,0:T(8,128)(2,1)S(1)} %copy-done.3), custom_call_target="tpu_custom_call" | custom-call | tf_op jit(solution)/shard_map/spread_and_gather/pallas_call | solution.py:157
  43.2 0.0 copy-start.4
  43.2 0.6 copy-done.4
  43.8 0.0 copy-start.5
  43.8 0.7 copy-done.5
  44.5 10.5 %attend.1 = (bf16[2,4,128,512]{3,2,1,0:T(8,128)(2,1)S(1)}, f32[2,4,1,512]{3,2,1,0:T(1,128)S(1)}) custom-call(s32[64]{0:T(128)S(1)} %copy-done.4, s32[64]{0:T(128)S(1)} %copy-done.5, bf16[2,4,512,128]{3,2,1,0:T(8,128)(2,1)S(1)} %get-tuple-element.6.q, bf16[4,4,2,512,128]{4,3,2,1,0:T(8,128)(2,1)S(1)} %get-tuple-element.7.kv), custom_call_target="tpu_custom_call" | custom-call | tf_op jit(solution)/shard_map/attend/pallas_call | solution.py:319
  55.0 0.0 copy-done
  55.0 43.3 %return_and_project.1 = (bf16[512,1024]{1,0:T(8,128)(2,1)S(1)}, f32[4,512]{1,0:T(4,128)S(1)}) custom-call(bf16[2,4,128,512]{3,2,1,0:T(8,128)(2,1)S(1)} %get-tuple-element.8.o, f32[2,4,1,512]{3,2,1,0:T(1,128)S(1)} %get-tuple-element.9.logs, bf16[512,4096]{1,0:T(8,128)(2,1)S(1)} %copy-done), custom_call_target="tpu_custom_call" | custom-call | tf_op jit(solution)/shard_map/return_and_project/pallas_call | solution.py:471
  98.4 1.0 copy.10
  99.3 0.6 copy.11
Async XLA Ops:
  0.6 54.4 %copy-start = (bf16[512,4096]{1,0:T(8,128)(2,1)S(1)}, bf16[512,4096]{1,0:T(8,128)(2,1)}, u32[]{:S(2)}) copy-start(bf16[512,4096]{1,0:T(8,128)(2,1)} %w.1) | copy-start | bytes 12582916
  0.6 1.2 %copy-start.1 = (bf16[512,512]{1,0:T(8,128)(2,1)S(1)}, bf16[512,512]{1,0:T(8,128)(2,1)}, u32[]{:S(2)}) copy-start(bf16[512,512]{1,0:T(8,128)(2,1)} %q.1) | copy-start | bytes 1572868
  1.8 1.3 %copy-start.2 = (bf16[512,512]{1,0:T(8,128)(2,1)S(1)}, bf16[512,512]{1,0:T(8,128)(2,1)}, u32[]{:S(2)}) copy-start(bf16[512,512]{1,0:T(8,128)(2,1)} %k.1) | copy-start | bytes 1572868
  3.1 1.0 %copy-start.3 = (bf16[512,512]{1,0:T(8,128)(2,1)S(1)}, bf16[512,512]{1,0:T(8,128)(2,1)}, u32[]{:S(2)}) copy-start(bf16[512,512]{1,0:T(8,128)(2,1)} %v.1) | copy-start | bytes 1572868
  43.2 0.7 copy-start.4
  43.8 0.7 copy-start.5

commit v3 on v2

--- a/solution.py
+++ b/solution.py
@@ -13,6 +13,7 @@
 LOG2E = math.log2(math.e)
 STREAMS = 4
 LEAST = -1e29
+PART = 128
 VMEM_BYTES = 40 * 1024 * 1024
 
 
@@ -41,6 +42,9 @@
         self.p, self.r, self.y = split_ctx(self.ctx, self.core)
         self.pair, self.bit = lax.div(self.p, 2), pair_bit(self.p)
         self.m = self.y * 2 + self.bit
+        self.mate = self.high * 2 + 1 - self.core
+        self.across = (1 - self.high) * 2 + self.core
+        self.diagonal = (1 - self.high) * 2 + 1 - self.core
 
     def member(self, i):
         bit = 1 - self.bit if i % 2 else self.bit
@@ -53,6 +57,9 @@
 
     def at_ring(self, r):
         return (ctx_of(self.core, self.p, r, self.y), self.tp)
+
+    def at_tp(self, tp):
+        return (self.ctx, tp)
 
     def at_twin(self):
         return (ctx_of(self.core, 3 - self.p, self.r, self.y), self.tp)
@@ -76,18 +83,29 @@
     return lambda: pl.semaphore_wait(barrier, len(partners))
 
 
-def gather_kernel(q, k, v, qh, kv, own_sem, s_send, s_recv, g_send, g_recv, t_send, t_recv):
+def gather_kernel(
+    q, k, v, w, qh, kv, w_near, w_far,
+    own_sem, s_send, s_recv, g_send, g_recv, t_send, t_recv, w_send, w_recv,
+):
     me = Place()
     left, right = lax.rem(me.r + 3, 4), lax.rem(me.r + 1, 4)
     wait_all = greet(
         [me.at_member(me.member(i)) for i in (1, 2, 3)]
-        + [me.at_ring(left), me.at_ring(right), me.at_twin()]
+        + [me.at_ring(left), me.at_ring(right), me.at_twin(), me.at_tp(me.mate)]
+        + [me.at_tp(me.across), me.at_tp(me.diagonal)]
     )
     mine = head_columns(me.m)
+    columns = w_near.shape[2]
+    quarter = w_far.shape[1]
+
+    def weight_columns(tp):
+        return pl.ds(pl.multiple_of(tp * columns, columns), columns)
+
     own = [
         pltpu.make_async_copy(k.at[:, mine], kv.at[me.r, me.m, 0], own_sem.at[0]),
         pltpu.make_async_copy(v.at[:, mine], kv.at[me.r, me.m, 1], own_sem.at[1]),
         pltpu.make_async_copy(q.at[:, mine], qh.at[me.pair, me.m], own_sem.at[2]),
+        pltpu.make_async_copy(w.at[:, weight_columns(me.tp)], w_near.at[0], own_sem.at[3]),
     ]
     for copy in own:
         copy.start()
@@ -118,6 +136,18 @@
     def arrived(i, j, rel):
         ring(i, j, rel, me.r, right).wait_recv()
 
+    def weights_across(n):
+        to = (me.across, me.diagonal)[n]
+        place = (me.r, me.p)[n]
+        rows = pl.ds(pl.multiple_of(place * quarter, quarter), quarter)
+        return remote(
+            w.at[rows, weight_columns(to)], w_far.at[me.core],
+            w_send.at[n], w_recv.at[n], me.at_tp(to),
+        )
+
+    weights_to_mate = remote(
+        w.at[:, weight_columns(me.mate)], w_near.at[1], w_send.at[2], w_recv.at[2], me.at_tp(me.mate)
+    )
     for a in (0, 1, 2):
         for i in (1, 2, 3):
             start(spread(i, a))
@@ -135,7 +165,12 @@
             start(ring(i - 1, 0, 2, left, right))
             arrived(i - 1, 1, 1)
             start(ring(i - 1, 1, 2, right, left))
+        if i == 3:
+            start(weights_across(0))
+            start(weights_across(1))
+            start(weights_to_mate)
     own[2].wait()
+    own[3].wait()
     start(twin(0))
     for i in (1, 2, 3):
         spread(i, 2).wait_recv()
@@ -146,12 +181,15 @@
         arrived(i, 0, 2)
         arrived(i, 1, 2)
         twin(i).wait_recv()
+    weights_across(0).wait_recv()
+    weights_across(1).wait_recv()
+    weights_to_mate.wait_recv()
     for copy in sends:
         copy.wait_send()
 
 
-def gather(q, k, v):
-    rows = q.shape[0]
+def gather(q, k, v, w):
+    rows, depth, columns = q.shape[0], w.shape[0], w.shape[1] // 4
     anywhere, near = pl.BlockSpec(memory_space=pltpu.HBM), pl.BlockSpec(memory_space=pltpu.VMEM)
     dma = pltpu.SemaphoreType.DMA
     return pl.pallas_call(
@@ -160,16 +198,19 @@
         out_shape=(
             jax.ShapeDtypeStruct((2, 4, rows, HEAD), q.dtype),
             jax.ShapeDtypeStruct((4, 4, 2, rows, HEAD), q.dtype),
+            jax.ShapeDtypeStruct((2, depth, columns), w.dtype),
+            jax.ShapeDtypeStruct((2, depth // 4, columns), w.dtype),
         ),
-        in_specs=[anywhere] * 3,
-        out_specs=(near, near),
+        in_specs=[anywhere] * 4,
+        out_specs=(near,) * 4,
         scratch_shapes=[
-            dma((3,)), dma((3, 3)), dma((3, 3)), dma((4, 2, 3)), dma((4, 2, 3)), dma((4,)), dma((4,)),
+            dma((4,)), dma((3, 3)), dma((3, 3)), dma((4, 2, 3)), dma((4, 2, 3)), dma((4,)), dma((4,)),
+            dma((3,)), dma((3,)),
         ],
         compiler_params=pltpu.CompilerParams(
             collective_id=0, has_side_effects=True, vmem_limit_bytes=VMEM_BYTES
         ),
-    )(q, k, v)
+    )(q, k, v, w)
 
 
 def attend_kernel(
@@ -305,7 +346,10 @@
         rows = pl.ds(pl.multiple_of(lax.rem(u, 2) * half, half), half)
         some = total[u] > 0.0
         safe = jnp.where(some, total[u], 1.0)
-        out[at[0], at[1], :, rows] = (summed[u] * (1.0 / safe)).astype(out.dtype)
+        attended = (summed[u] * (1.0 / safe)).astype(out.dtype)
+        for e in range(half // PART):
+            chunk = lax.rem(u, 2) * (half // PART) + e
+            out[at[0], at[1], chunk] = attended[:, e * PART : (e + 1) * PART]
         logs[at[0], at[1], :, rows] = jnp.where(some, top[u] * SCALE + jnp.log(safe), -1e30)
         return 0
 
@@ -320,7 +364,7 @@
         attend_kernel,
         name="attend",
         out_shape=(
-            jax.ShapeDtypeStruct((2, 4, HEAD, rows), q.dtype),
+            jax.ShapeDtypeStruct((2, 4, rows // PART, HEAD, PART), q.dtype),
             jax.ShapeDtypeStruct((2, 4, 1, rows), jnp.float32),
         ),
         in_specs=[far, far, near, near],
@@ -343,23 +387,25 @@
     )(lengths, layout, q, kv)
 
 
-CHUNKS = 4
-
-
 def project_kernel(
-    o, logs, w, mixed, log_out,
-    o_in, lo_in, merged, merged_logs, att, logs_in, own_sum, c_out, c_in, y_out, y_in,
-    b_send, b_recv, lb_sem, a_send, a_recv, l_send, l_recv, c_send, c_recv, y_send, y_recv,
+    o, logs, w_near, w_quarter, mixed, log_out,
+    o_in, lo_in, merged, merged_logs, att, att_in, logs_in, w_far, total,
+    own_sem, b_send, b_recv, lb_sem, a_send, a_recv, l_send, l_recv, x_send, x_recv, w_send, w_recv,
 ):
     me = Place()
-    rows, columns = mixed.shape
-    part = rows // CHUNKS
-    high, core = me.high, me.core
-    targets = ((1 - high) * 2 + 1 - core, (1 - high) * 2 + core, high * 2 + 1 - core, me.tp)
-    mate, across = (me.ctx, targets[2]), (me.ctx, targets[1])
-    greet(
-        [me.at_member(me.member(i)) for i in (1, 2, 3)] + [me.at_twin(), mate, across]
-    )()
+    chunks = o.shape[2]
+    left, right = lax.rem(me.r + 3, 4), lax.rem(me.r + 1, 4)
+    wait_all = greet(
+        [me.at_member(me.member(i)) for i in (1, 2, 3)]
+        + [me.at_ring(left), me.at_ring(right), me.at_twin()]
+        + [me.at_tp(me.mate), me.at_tp(me.across)]
+    )
+    own = [
+        pltpu.make_async_copy(w_quarter.at[n], w_far.at[n, me.r], own_sem.at[n]) for n in (0, 1)
+    ]
+    for copy in own:
+        copy.start()
+    wait_all()
     sends = []
 
     def start(copy):
@@ -368,30 +414,44 @@
 
     order = (3, 1, 2, 0)
 
-    def to_twin(i):
-        m = me.member(i)
-        return remote(o.at[1 - me.pair, m], o_in.at[m], b_send.at[i], b_recv.at[i], me.at_twin())
-
-    def to_owner(i):
+    def to_twin(i, c):
         m = me.member(i)
         return remote(
-            merged.at[i - 1], att.at[:, head_columns(me.m)],
-            a_send.at[i - 1], a_recv.at[i - 1], me.at_member(m),
+            o.at[1 - me.pair, m, c], o_in.at[m, c], b_send.at[i, c], b_recv.at[i, c], me.at_twin()
+        )
+
+    def to_owner(i, c):
+        return remote(
+            merged.at[i - 1, c], att.at[c, :, head_columns(me.m)],
+            a_send.at[i - 1, c], a_recv.at[i - 1, c], me.at_member(me.member(i)),
         )
 
     def log_to_owner(i):
-        m = me.member(i)
         return remote(
-            merged_logs.at[i - 1], logs_in.at[me.m],
-            l_send.at[i - 1], l_recv.at[i - 1], me.at_member(m),
-        )
+            merged_logs.at[i], logs_in.at[me.m],
+            l_send.at[i - 1], l_recv.at[i - 1], me.at_member(me.member(i)),
+        )
+
+    def pass_att(n, c):
+        src = att_in.at[0, c] if n == 2 else att.at[c]
+        to = me.across if n == 0 else me.mate
+        return remote(src, att_in.at[n, c], x_send.at[n, c], x_recv.at[n, c], me.at_tp(to))
+
+    def weights(n, rel, origin, to):
+        slot = w_far.at[n, origin]
+        return remote(slot, slot, w_send.at[n, rel], w_recv.at[n, rel], me.at_ring(to))
+
+    def weights_arrived(n, rel):
+        weights(n, rel, me.r, right).wait_recv()
 
     twin_logs = remote(logs.at[1 - me.pair], lo_in, lb_sem.at[0], lb_sem.at[1], me.at_twin())
     start(twin_logs)
-    for i in order:
-        start(to_twin(i))
+    for c in range(chunks):
+        for i in order:
+            start(to_twin(i, c))
     twin_logs.wait_recv()
-    for i in order:
+    shares = []
+    for i in range(4):
         m = me.member(i)
         one, two = logs[me.pair, m], lo_in[m]
         most = jnp.maximum(one, two)
@@ -399,73 +459,91 @@
         both = e_one + e_two
         final = most + jnp.log(both)
         share = 1.0 / both
-        to_twin(i).wait_recv()
-        whole = o[me.pair, m].astype(jnp.float32) * (e_one * share) + o_in[m].astype(
-            jnp.float32
-        ) * (e_two * share)
-        turned = whole.T.astype(jnp.bfloat16)
+        shares.append((e_one * share, e_two * share))
         if i == 0:
-            att[:, head_columns(me.m)] = turned
             logs_in[me.m] = final
         else:
-            merged[i - 1] = turned
-            merged_logs[i - 1] = final
-            start(to_owner(i))
+            merged_logs[i] = final
             start(log_to_owner(i))
-    for i in (1, 2, 3):
-        to_owner(i).wait_recv()
-
-    def chunk(c):
-        return pl.ds(c * part, part)
-
-    def product(c, n):
-        at = pl.ds(pl.multiple_of(targets[n] * columns, columns), columns)
-        return jnp.dot(att[chunk(c), :], w[:, at], preferred_element_type=jnp.float32)
-
-    def to_mate(c, n):
-        return remote(
-            c_out.at[n, chunk(c)], c_in.at[n, chunk(c)], c_send.at[n, c], c_recv.at[n, c], mate
-        )
-
-    def to_across(c):
-        return remote(y_out.at[chunk(c)], y_in.at[chunk(c)], y_send.at[c], y_recv.at[c], across)
-
-    def give(c, n):
-        c_out[n, chunk(c), :] = product(c, 2 * n).astype(jnp.bfloat16)
-        start(to_mate(c, n))
-
-    def pass_on(c):
-        mine = product(c, 1)
-        to_mate(c, 0).wait_recv()
-        y_out[chunk(c), :] = (mine + c_in[0, chunk(c), :].astype(jnp.float32)).astype(jnp.bfloat16)
-        start(to_across(c))
-
-    give(0, 0)
-    for c in range(CHUNKS):
-        if c + 1 < CHUNKS:
-            give(c + 1, 0)
-        pass_on(c)
-    for c in range(CHUNKS):
-        give(c, 1)
-    for c in range(CHUNKS):
-        mine = product(c, 3)
-        to_mate(c, 1).wait_recv()
-        own_sum[chunk(c), :] = mine + c_in[1, chunk(c), :].astype(jnp.float32)
+
+    def merge(c):
+        for i in order:
+            m = me.member(i)
+            lanes = slice(c * PART, (c + 1) * PART)
+            to_twin(i, c).wait_recv()
+            whole = (
+                o[me.pair, m, c].astype(jnp.float32) * shares[i][0][:, lanes]
+                + o_in[m, c].astype(jnp.float32) * shares[i][1][:, lanes]
+            )
+            turned = whole.T.astype(jnp.bfloat16)
+            if i == 0:
+                att[c, :, head_columns(me.m)] = turned
+            else:
+                merged[i - 1, c] = turned
+                start(to_owner(i, c))
+
+    def share_out(c):
+        for i in (1, 2, 3):
+            to_owner(i, c).wait_recv()
+        start(pass_att(0, c))
+        start(pass_att(1, c))
+        total[c] = jnp.dot(att[c], w_near[0], preferred_element_type=jnp.float32)
+
+    def far_weights(n):
+        return w_far[n].reshape(w_near.shape[1:])
+
+    def cross(c):
+        pass_att(1, c).wait_recv()
+        total[c] += jnp.dot(att_in[1, c], w_near[1], preferred_element_type=jnp.float32)
+        pass_att(0, c).wait_recv()
+        start(pass_att(2, c))
+
+    def finish(c):
+        both = total[c] + jnp.dot(
+            att_in[0, c], far_weights(me.core), preferred_element_type=jnp.float32
+        )
+        pass_att(2, c).wait_recv()
+        both += jnp.dot(
+            att_in[2, c], far_weights(1 - me.core), preferred_element_type=jnp.float32
+        )
+        mixed[c * PART : (c + 1) * PART, :] = both.astype(mixed.dtype)
+
+    for t in range(chunks + 3):
+        if t < chunks:
+            merge(t)
+        if t == 0:
+            for n in (0, 1):
+                own[n].wait()
+                start(weights(n, 0, me.r, right))
+                start(weights(n, 1, me.r, left))
+        if 0 <= t - 1 < chunks:
+            share_out(t - 1)
+        if t == 3:
+            weights_arrived(0, 0)
+            start(weights(0, 2, left, right))
+            weights_arrived(1, 1)
+            start(weights(1, 2, right, left))
+        if 0 <= t - 2 < chunks:
+            cross(t - 2)
+        if t == chunks + 1:
+            weights_arrived(0, 1)
+            weights_arrived(1, 0)
+            weights_arrived(0, 2)
+            weights_arrived(1, 2)
+            for c in range(chunks - 1):
+                finish(c)
+    finish(chunks - 1)
     for i in (1, 2, 3):
         log_to_owner(i).wait_recv()
     for h in range(4):
         log_out[h : h + 1, :] = logs_in[h]
-    for c in range(CHUNKS):
-        to_across(c).wait_recv()
-        mixed[chunk(c), :] = (own_sum[chunk(c), :] + y_in[chunk(c), :].astype(jnp.float32)).astype(
-            jnp.bfloat16
-        )
     for copy in sends:
         copy.wait_send()
 
 
-def project(o, logs, w):
-    rows, depth, columns = o.shape[3], w.shape[0], w.shape[1] // 4
+def project(o, logs, w_near, w_quarter):
+    chunks, depth, columns = o.shape[2], w_near.shape[1], w_near.shape[2]
+    rows = chunks * PART
     near = pl.BlockSpec(memory_space=pltpu.VMEM)
     dma = pltpu.SemaphoreType.DMA
     return pl.pallas_call(
@@ -475,33 +553,33 @@
             jax.ShapeDtypeStruct((rows, columns), jnp.bfloat16),
             jax.ShapeDtypeStruct((4, rows), jnp.float32),
         ),
-        in_specs=[near, near, near],
+        in_specs=[near] * 4,
         out_specs=(near, near),
         scratch_shapes=[
-            pltpu.VMEM((4, HEAD, rows), jnp.bfloat16),
+            pltpu.VMEM((4, chunks, HEAD, PART), jnp.bfloat16),
             pltpu.VMEM((4, 1, rows), jnp.float32),
-            pltpu.VMEM((3, rows, HEAD), jnp.bfloat16),
-            pltpu.VMEM((3, 1, rows), jnp.float32),
-            pltpu.VMEM((rows, depth), jnp.bfloat16),
+            pltpu.VMEM((3, chunks, PART, HEAD), jnp.bfloat16),
             pltpu.VMEM((4, 1, rows), jnp.float32),
-            pltpu.VMEM((rows, columns), jnp.float32),
-            pltpu.VMEM((2, rows, columns), jnp.bfloat16),
-            pltpu.VMEM((2, rows, columns), jnp.bfloat16),
-            pltpu.VMEM((rows, columns), jnp.bfloat16),
-            pltpu.VMEM((rows, columns), jnp.bfloat16),
-            dma((4,)), dma((4,)), dma((2,)), dma((3,)), dma((3,)), dma((3,)), dma((3,)),
-            dma((2, CHUNKS)), dma((2, CHUNKS)), dma((CHUNKS,)), dma((CHUNKS,)),
+            pltpu.VMEM((chunks, PART, depth), jnp.bfloat16),
+            pltpu.VMEM((3, chunks, PART, depth), jnp.bfloat16),
+            pltpu.VMEM((4, 1, rows), jnp.float32),
+            pltpu.VMEM((2, 4, depth // 4, columns), jnp.bfloat16),
+            pltpu.VMEM((chunks, PART, columns), jnp.float32),
+            dma((2,)), dma((4, chunks)), dma((4, chunks)), dma((2,)), dma((3, chunks)),
+            dma((3, chunks)), dma((3,)), dma((3,)), dma((3, chunks)), dma((3, chunks)),
+            dma((2, 3)), dma((2, 3)),
         ],
         compiler_params=pltpu.CompilerParams(
             collective_id=1, has_side_effects=True, vmem_limit_bytes=VMEM_BYTES
         ),
-    )(o, logs, w)
+    )(o, logs, w_near, w_quarter)
 
 
 def local(queries, keys, values, out_weight, doc_lengths, layout):
-    qh, kv = gather(queries, keys, values)
+    queries, keys, values, out_weight = (pltpu.with_memory_space_constraint(t, pltpu.HBM) for t in (queries, keys, values, out_weight))
+    qh, kv, w_near, w_quarter = gather(queries, keys, values, out_weight)
     o, logs = attend(doc_lengths, layout, qh, kv)
-    return project(o, logs, out_weight)
+    return project(o, logs, w_near, w_quarter)
 
 
 def solution(mesh):

time: 100 us -> 84.1 us (0.84)
  Pallas kernels: 92.9 us -> 81.7 us
  local copies, waits for them, and re-layouts: 6.36 us -> 1.58 us
    pallas_call x1, Pallas kernels: 43.3 us -> 29.5 us  [project(): pl.pallas_call(project_kernel, name='return_and_project', out_shape=(jax....]
    unnamed x14 -> x6, local copies, waits for them, and re-layouts: 6.36 us -> 1.58 us
    pallas_call x1, Pallas kernels: 39 us -> 40.7 us  [gather(): pl.pallas_call(gather_kernel, name='spread_and_gather', out_shape=(jax.Sh...]
    pallas_call x1, Pallas kernels: 10.5 us -> 11.5 us  [attend(): pl.pallas_call(attend_kernel, name='attend', out_shape=(jax.ShapeDtypeStr...]
where the time goes in v3:
time: 84.1 us; the launch traced here: 84 us
  Pallas kernels  81.7 us (97%)
  local copies, waits for them, and re-layouts  1.58 us (2%)
    pallas_call x1, Pallas kernels, gather(): pl.pallas_call(gather_kernel, name='spread_and_gather', out_shape=(jax.Sh...  40.7 us
    pallas_call x1, Pallas kernels, project(): pl.pallas_call(project_kernel, name='return_and_project', out_shape=(jax....  29.5 us
    pallas_call x1, Pallas kernels, attend(): pl.pallas_call(attend_kernel, name='attend', out_shape=(jax.ShapeDtypeStr...  11.5 us

profile of v3, /device:TPU:1, one launch (start us, length us, event | category | flops | bytes accessed | tf_op | source)
XLA Modules:
  0.0 84.0 jit_solution(8806473588721378463)
XLA Ops:
  0.6 0.0 copy-start.1
  0.6 0.0 copy-start
  0.7 40.7 %spread_and_gather.1 = (bf16[2,4,512,128]{3,2,1,0:T(8,128)(2,1)S(1)}, bf16[4,4,2,512,128]{4,3,2,1,0:T(8,128)(2,1)S(1)}, bf16[2,512,1024]{2,1,0:T(8,128)(2,1)S(1)}, bf16[2,128,1024]{2,1,0:T(8,128)(2,1)S(1)}) custom-call(bf16[512,512]{1,0:T(8,128)(2,1)} %q.1, bf16[512,512]{1,0:T(8,128)(2,1)} %k.1, bf16[512,512]{1,0:T(8,128)(2,1)} %v.1, bf16[512,4096]{1,0:T(8,128)(2,1)} %w.1), custom_call_target="tpu_custom_call" | custom-call | tf_op jit(solution)/shard_map/spread_and_gather/pallas_call | solution.py:195
  41.4 0.0 copy-done.1
  41.4 0.0 copy-done
  41.4 11.5 %attend.1 = (bf16[2,4,4,128,128]{4,3,2,1,0:T(8,128)(2,1)S(1)}, f32[2,4,1,512]{3,2,1,0:T(1,128)S(1)}) custom-call(s32[64]{0:T(128)S(1)} %copy-done, s32[64]{0:T(128)S(1)} %copy-done.1, bf16[2,4,512,128]{3,2,1,0:T(8,128)(2,1)S(1)} %get-tuple-element.8.q, bf16[4,4,2,512,128]{4,3,2,1,0:T(8,128)(2,1)S(1)} %get-tuple-element.9.kv), custom_call_target="tpu_custom_call" | custom-call | tf_op jit(solution)/shard_map/attend/pallas_call | solution.py:363
  53.0 29.5 %return_and_project.1 = (bf16[512,1024]{1,0:T(8,128)(2,1)S(1)}, f32[4,512]{1,0:T(4,128)S(1)}) custom-call(bf16[2,4,4,128,128]{4,3,2,1,0:T(8,128)(2,1)S(1)} %get-tuple-element.10.o, f32[2,4,1,512]{3,2,1,0:T(1,128)S(1)} %get-tuple-element.11.logs, bf16[2,512,1024]{2,1,0:T(8,128)(2,1)S(1)} %get-tuple-element.12.w_near, ...), custom_call_target="tpu_custom_call" | custom-call | tf_op jit(solution)/shard_map/return_and_project/pallas_call | solution.py:549
  82.4 1.0 %copy.10 = bf16[512,1024]{1,0:T(8,128)(2,1)} copy(bf16[512,1024]{1,0:T(8,128)(2,1)S(1)} %get-tuple-element.16) | data formatting | bytes 2097152
  83.4 0.6 copy.11
Async XLA Ops:
  0.6 40.8 %copy-start.1 = (s32[64]{0:T(128)S(1)}, s32[64]{0:T(128)}, u32[]{:S(2)}) copy-start(s32[64]{0:T(128)} %far_layout.1) | copy-start | bytes 772
  0.6 40.8 %copy-start = (s32[64]{0:T(128)S(1)}, s32[64]{0:T(128)}, u32[]{:S(2)}) copy-start(s32[64]{0:T(128)} %far_lengths.1) | copy-start | bytes 772

commit v4 on v3

--- a/solution.py
+++ b/solution.py
@@ -14,6 +14,7 @@
 STREAMS = 4
 LEAST = -1e29
 PART = 128
+BLOCKS = 64
 VMEM_BYTES = 40 * 1024 * 1024
 
 
@@ -84,8 +85,8 @@
 
 
 def gather_kernel(
-    q, k, v, w, qh, kv, w_near, w_far,
-    own_sem, s_send, s_recv, g_send, g_recv, t_send, t_recv, w_send, w_recv,
+    q, k, v, w, far_lengths, far_layout, qh, kv, w_near, w_far, table, lows,
+    lengths, layout, table_sem, own_sem, s_send, s_recv, g_send, g_recv, t_send, t_recv, w_send, w_recv,
 ):
     me = Place()
     left, right = lax.rem(me.r + 3, 4), lax.rem(me.r + 1, 4)
@@ -107,6 +108,10 @@
         pltpu.make_async_copy(q.at[:, mine], qh.at[me.pair, me.m], own_sem.at[2]),
         pltpu.make_async_copy(w.at[:, weight_columns(me.tp)], w_near.at[0], own_sem.at[3]),
     ]
+    own += [
+        pltpu.make_async_copy(far_lengths, lengths, table_sem.at[0]),
+        pltpu.make_async_copy(far_layout, layout, table_sem.at[1]),
+    ]
     for copy in own:
         copy.start()
     wait_all()
@@ -116,6 +121,39 @@
     def start(copy):
         copy.start()
         sends.append(copy)
+
+    def make_tables():
+        own[4].wait()
+        own[5].wait()
+        half = lows.shape[1]
+        lane = lax.broadcasted_iota(jnp.int32, (1, table.shape[1]), 1)
+        row = lax.broadcasted_iota(jnp.int32, lows.shape, 0)
+        q_pos = lax.broadcasted_iota(jnp.int32, lows.shape, 1)
+        for u in range(16):
+            p, y = member_place(u // 8, u // 2 % 4)
+            block = layout[ctx_of(me.core, p, me.r, y) * 2 + u % 2]
+            q_pos += jnp.where(row == u, block * half, 0)
+
+        def place(b, state):
+            where_is, held = state
+            block = layout[b]
+            return jnp.where(lane == block, b, where_is), jnp.where(lane == b, block, held)
+
+        def walk(j, state):
+            at, first, low = state
+            first = jnp.where(lane * half >= at, at, first)
+            low = jnp.where(q_pos >= at, at, low)
+            return at + lengths[j], first, low
+
+        none = jnp.zeros_like(lane)
+        where_is, held = lax.fori_loop(0, layout.shape[0], place, (none, none))
+        _, first, low = lax.fori_loop(
+            0, lengths.shape[0], walk, (jnp.int32(0), none, jnp.zeros_like(q_pos))
+        )
+        table[0:1, :] = where_is
+        table[1:2, :] = first
+        table[2:3, :] = held
+        lows[...] = low
 
     def spread(i, a):
         to = me.member(i)
@@ -148,9 +186,22 @@
     weights_to_mate = remote(
         w.at[:, weight_columns(me.mate)], w_near.at[1], w_send.at[2], w_recv.at[2], me.at_tp(me.mate)
     )
-    for a in (0, 1, 2):
-        for i in (1, 2, 3):
+    for a in (2, 0, 1):
+        for i in (2, 3, 1):
             start(spread(i, a))
+
+    def pass_query(i):
+        if i == 0:
+            own[2].wait()
+        else:
+            spread(i, 2).wait_recv()
+        start(twin(i))
+
+    def pass_weights():
+        start(weights_across(0))
+        start(weights_across(1))
+        start(weights_to_mate)
+
     for i in range(5):
         if i < 4:
             for j in (0, 1):
@@ -160,21 +211,21 @@
                     spread(i, j).wait_recv()
                 start(ring(i, j, 0, me.r, right))
                 start(ring(i, j, 1, me.r, left))
+        if i == 0:
+            pass_query(0)
+            make_tables()
+            pass_query(1)
+        if i == 1:
+            pass_query(2)
+            pass_query(3)
+        if i == 2:
+            pass_weights()
         if i >= 1:
             arrived(i - 1, 0, 0)
             start(ring(i - 1, 0, 2, left, right))
             arrived(i - 1, 1, 1)
             start(ring(i - 1, 1, 2, right, left))
-        if i == 3:
-            start(weights_across(0))
-            start(weights_across(1))
-            start(weights_to_mate)
-    own[2].wait()
     own[3].wait()
-    start(twin(0))
-    for i in (1, 2, 3):
-        spread(i, 2).wait_recv()
-        start(twin(i))
     for i in range(4):
         arrived(i, 0, 1)
         arrived(i, 1, 0)
@@ -188,7 +239,7 @@
         copy.wait_send()
 
 
-def gather(q, k, v, w):
+def gather(q, k, v, w, lengths, layout):
     rows, depth, columns = q.shape[0], w.shape[0], w.shape[1] // 4
     anywhere, near = pl.BlockSpec(memory_space=pltpu.HBM), pl.BlockSpec(memory_space=pltpu.VMEM)
     dma = pltpu.SemaphoreType.DMA
@@ -200,94 +251,59 @@
             jax.ShapeDtypeStruct((4, 4, 2, rows, HEAD), q.dtype),
             jax.ShapeDtypeStruct((2, depth, columns), w.dtype),
             jax.ShapeDtypeStruct((2, depth // 4, columns), w.dtype),
+            jax.ShapeDtypeStruct((8, 128), jnp.int32),
+            jax.ShapeDtypeStruct((16, rows // 2), jnp.int32),
         ),
-        in_specs=[anywhere] * 4,
-        out_specs=(near,) * 4,
+        in_specs=[anywhere] * 6,
+        out_specs=(near,) * 6,
         scratch_shapes=[
+            pltpu.SMEM(lengths.shape, jnp.int32),
+            pltpu.SMEM(layout.shape, jnp.int32),
+            dma((2,)),
             dma((4,)), dma((3, 3)), dma((3, 3)), dma((4, 2, 3)), dma((4, 2, 3)), dma((4,)), dma((4,)),
             dma((3,)), dma((3,)),
         ],
         compiler_params=pltpu.CompilerParams(
             collective_id=0, has_side_effects=True, vmem_limit_bytes=VMEM_BYTES
         ),
-    )(q, k, v, w)
+    )(q, k, v, w, lengths, layout)
 
 
 def attend_kernel(
-    far_lengths, far_layout, q, kv, out, logs,
-    lengths, layout, start, where_is, doc_at, work, count, lows, top, total, summed, table_sem,
+    near_table, lows, q, kv, out, logs, table, work, count, top, total, summed, table_sem
 ):
     me = Place()
-    tables = [
-        pltpu.make_async_copy(far_lengths, lengths, table_sem.at[0]),
-        pltpu.make_async_copy(far_layout, layout, table_sem.at[1]),
-    ]
-    for copy in tables:
-        copy.start()
+    blocks = BLOCKS
+    half = q.shape[2] // 2
+    spare = 16
+    fetch = pltpu.make_async_copy(near_table, table, table_sem.at[0])
+    fetch.start()
     top[...] = jnp.full(top.shape, LEAST, jnp.float32)
     total[...] = jnp.zeros(total.shape, jnp.float32)
-    for copy in tables:
-        copy.wait()
-    blocks, docs = layout.shape[0], lengths.shape[0]
-    half = q.shape[2] // 2
-    spare = 16
-
-    def place(b, _):
-        where_is[layout[b]] = b
-        return 0
-
-    lax.fori_loop(0, blocks, place, 0)
-
-    def walk(j, at):
-        start[j] = at
-        end = at + lengths[j]
-
-        def mark(b, _):
-            doc_at[b] = j
-            return 0
-
-        lax.fori_loop(lax.div(at + half - 1, half), lax.div(end + half - 1, half), mark, 0)
-        return end
-
-    start[docs] = lax.fori_loop(0, docs, walk, 0)
+    summed[...] = jnp.zeros(summed.shape, jnp.float32)
     for n in range(STREAMS):
         count[n] = 0
+    fetch.wait()
 
     def query_block(u):
         p, y = member_place(lax.div(u, 8), lax.rem(lax.div(u, 2), 4))
-        return layout[ctx_of(me.core, p, me.r, y) * 2 + lax.rem(u, 2)]
+        return table[2, ctx_of(me.core, p, me.r, y) * 2 + lax.rem(u, 2)]
 
     def plan(u, _):
         block = query_block(u)
-        base = block * half
-        first_doc = doc_at[block]
-        q_pos = base + lax.broadcasted_iota(jnp.int32, (1, half), 1)
-
-        def doc_start(state):
-            j, low = state
-            at = start[j]
-            return j + 1, jnp.where(q_pos >= at, at, low)
-
-        _, low = lax.while_loop(
-            lambda state: start[state[0]] < base + half,
-            doc_start,
-            (first_doc + 1, jnp.full((1, half), start[first_doc], jnp.int32)),
-        )
-        lows[u] = low
-        summed[u] = jnp.zeros((HEAD, half), jnp.float32)
         stream = jnp.int32(0)
         for n in range(1, STREAMS):
             stream = jnp.where(count[n] < count[stream], n, stream)
 
         def add(key_block, filled):
-            at = where_is[key_block]
+            at = table[0, key_block]
             p, r, y = split_ctx(lax.div(at, 2), me.core)
             slot = r * 8 + (y * 2 + pair_bit(p)) * 2 + lax.rem(at, 2)
             work[stream, filled] = (u * blocks + key_block) * 32 + slot
             return filled + jnp.where(lax.div(p, 2) == me.pair, 1, 0)
 
         count[stream] = lax.fori_loop(
-            lax.div(start[first_doc], half), block + 1, add, count[stream]
+            lax.div(table[1, block], half), block + 1, add, count[stream]
         )
         return 0
 
@@ -317,7 +333,7 @@
             query = q[lax.div(real, 8), lax.rem(lax.div(real, 2), 4), q_rows, :]
             key, value = kv[r_k, m_k, 0, k_rows, :], kv[r_k, m_k, 1, k_rows, :]
             q_pos = query_block(real) * half + lax.broadcasted_iota(jnp.int32, (1, half), 1)
-            todo.append((u, key_block, query, key, value, q_pos, lows[real]))
+            todo.append((u, key_block, query, key, value, q_pos, lows[pl.ds(real, 1), :]))
         scores = [
             lax.dot_general(key, query, (((1,), (1,)), ((), ())), preferred_element_type=jnp.float32)
             for _, _, query, key, _, _, _ in todo
@@ -356,10 +372,10 @@
     lax.fori_loop(0, 16, finish, 0)
 
 
-def attend(lengths, layout, q, kv):
-    rows, blocks = q.shape[2], layout.shape[0]
+def attend(table, lows, q, kv):
+    rows = q.shape[2]
     half = rows // 2
-    far, near = pl.BlockSpec(memory_space=pltpu.HBM), pl.BlockSpec(memory_space=pltpu.VMEM)
+    near = pl.BlockSpec(memory_space=pltpu.VMEM)
     return pl.pallas_call(
         attend_kernel,
         name="attend",
@@ -367,24 +383,19 @@
             jax.ShapeDtypeStruct((2, 4, rows // PART, HEAD, PART), q.dtype),
             jax.ShapeDtypeStruct((2, 4, 1, rows), jnp.float32),
         ),
-        in_specs=[far, far, near, near],
+        in_specs=[near] * 4,
         out_specs=(near, near),
         scratch_shapes=[
-            pltpu.SMEM(lengths.shape, jnp.int32),
-            pltpu.SMEM(layout.shape, jnp.int32),
-            pltpu.SMEM((lengths.shape[0] + 1,), jnp.int32),
-            pltpu.SMEM((blocks,), jnp.int32),
-            pltpu.SMEM((blocks,), jnp.int32),
-            pltpu.SMEM((STREAMS, 16 * blocks + 1), jnp.int32),
+            pltpu.SMEM(table.shape, jnp.int32),
+            pltpu.SMEM((STREAMS, 16 * BLOCKS + 1), jnp.int32),
             pltpu.SMEM((STREAMS,), jnp.int32),
-            pltpu.VMEM((16, 1, half), jnp.int32),
             pltpu.VMEM((16 + STREAMS, 1, half), jnp.float32),
             pltpu.VMEM((16 + STREAMS, 1, half), jnp.float32),
             pltpu.VMEM((16 + STREAMS, HEAD, half), jnp.float32),
-            pltpu.SemaphoreType.DMA((2,)),
+            pltpu.SemaphoreType.DMA((1,)),
         ],
         compiler_params=pltpu.CompilerParams(vmem_limit_bytes=VMEM_BYTES),
-    )(lengths, layout, q, kv)
+    )(table, lows, q, kv)
 
 
 def project_kernel(
@@ -576,9 +587,12 @@
 
 
 def local(queries, keys, values, out_weight, doc_lengths, layout):
-    queries, keys, values, out_weight = (pltpu.with_memory_space_constraint(t, pltpu.HBM) for t in (queries, keys, values, out_weight))
-    qh, kv, w_near, w_quarter = gather(queries, keys, values, out_weight)
-    o, logs = attend(doc_lengths, layout, qh, kv)
+    held = (
+        pltpu.with_memory_space_constraint(t, pltpu.HBM)
+        for t in (queries, keys, values, out_weight, doc_lengths, layout)
+    )
+    qh, kv, w_near, w_quarter, table, lows = gather(*held)
+    o, logs = attend(table, lows, qh, kv)
     return project(o, logs, w_near, w_quarter)
 
 

time: 84.1 us -> 81.8 us (0.973)
  Pallas kernels: 81.7 us -> 79.5 us
    pallas_call x1, Pallas kernels: 11.5 us -> 10.4 us  [attend(): pl.pallas_call(attend_kernel, name='attend', out_shape=(jax.ShapeDtypeStr...]
where the time goes in v4:
time: 81.8 us; the launch traced here: 81.7 us
  Pallas kernels  79.5 us (97%)
  local copies, waits for them, and re-layouts  1.57 us (2%)
    pallas_call x1, Pallas kernels, gather(): pl.pallas_call(gather_kernel, name='spread_and_gather', out_shape=(jax.Sh...  40 us
    pallas_call x1, Pallas kernels, project(): pl.pallas_call(project_kernel, name='return_and_project', out_shape=(jax....  29.1 us
    pallas_call x1, Pallas kernels, attend(): pl.pallas_call(attend_kernel, name='attend', out_shape=(jax.ShapeDtypeStr...  10.4 us

profile of v4, /device:TPU:1, one launch (start us, length us, event | category | flops | bytes accessed | tf_op | source)
XLA Modules:
  0.0 81.7 jit_solution(18085634323125081228)
XLA Ops:
  0.6 40.0 %spread_and_gather.1 = (bf16[2,4,512,128]{3,2,1,0:T(8,128)(2,1)S(1)}, bf16[4,4,2,512,128]{4,3,2,1,0:T(8,128)(2,1)S(1)}, bf16[2,512,1024]{2,1,0:T(8,128)(2,1)S(1)...) custom-call(bf16[512,512]{1,0:T(8,128)(2,1)} %q.1, bf16[512,512]{1,0:T(8,128)(2,1)} %k.1, ...), custom_call_target="tpu_custom_call" | custom-call | tf_op jit(solution)/shard_map/spread_and_gather/pallas_call | solution.py:246
  40.6 10.4 %attend.1 = (bf16[2,4,4,128,128]{4,3,2,1,0:T(8,128)(2,1)S(1)}, f32[2,4,1,512]{3,2,1,0:T(1,128)S(1)}) custom-call(s32[8,128]{1,0:T(8,128)S(1)} %get-tuple-element.10.near_table, s32[16,256]{1,0:T(8,128)S(1)} %get-tuple-element.11.lows, bf16[2,4,512,128]{3,2,1,0:T(8,128)(2,1)S(1)} %get-tuple-element.12.q, bf16[4,4,2,512,128]{4,3,2,1,0:T(8,128)(2,1)S(1)} %get-tuple-element.13.kv), custom_call_target="tpu_custom_call" | custom-call | tf_op jit(solution)/shard_map/attend/pallas_call | solution.py:379
  51.0 29.1 %return_and_project.1 = (bf16[512,1024]{1,0:T(8,128)(2,1)S(1)}, f32[4,512]{1,0:T(4,128)S(1)}) custom-call(bf16[2,4,4,128,128]{4,3,2,1,0:T(8,128)(2,1)S(1)} %get-tuple-element.14.o, f32[2,4,1,512]{3,2,1,0:T(1,128)S(1)} %get-tuple-element.15.logs, bf16[2,512,1024]{2,1,0:T(8,128)(2,1)S(1)} %get-tuple-element.16.w_near, ...), custom_call_target="tpu_custom_call" | custom-call | tf_op jit(solution)/shard_map/return_and_project/pallas_call | solution.py:560
  80.1 1.0 %copy.10 = bf16[512,1024]{1,0:T(8,128)(2,1)} copy(bf16[512,1024]{1,0:T(8,128)(2,1)S(1)} %get-tuple-element.20) | data formatting | bytes 2097152
  81.1 0.6 copy.11

commit v5 on v4

--- a/solution.py
+++ b/solution.py
@@ -13,7 +13,7 @@
 LOG2E = math.log2(math.e)
 STREAMS = 4
 LEAST = -1e29
-PART = 128
+PART = 256
 BLOCKS = 64
 VMEM_BYTES = 40 * 1024 * 1024
 
@@ -522,7 +522,7 @@
     for t in range(chunks + 3):
         if t < chunks:
             merge(t)
-        if t == 0:
+        if t == 1:
             for n in (0, 1):
                 own[n].wait()
                 start(weights(n, 0, me.r, right))

time: 81.8 us -> 80.9 us (0.989)
  Pallas kernels: 79.5 us -> 78.1 us
    pallas_call x1, Pallas kernels: 29.1 us -> 26.3 us  [project(): pl.pallas_call(project_kernel, name='return_and_project', out_shape=(jax....]
    pallas_call x1, Pallas kernels: 10.4 us -> 11.9 us  [attend(): pl.pallas_call(attend_kernel, name='attend', out_shape=(jax.ShapeDtypeStr...]
where the time goes in v5:
time: 80.9 us; the launch traced here: 80.4 us
  Pallas kernels  78.1 us (97%)
  local copies, waits for them, and re-layouts  1.57 us (2%)
    pallas_call x1, Pallas kernels, gather(): pl.pallas_call(gather_kernel, name='spread_and_gather', out_shape=(jax.Sh...  40 us
    pallas_call x1, Pallas kernels, project(): pl.pallas_call(project_kernel, name='return_and_project', out_shape=(jax....  26.3 us
    pallas_call x1, Pallas kernels, attend(): pl.pallas_call(attend_kernel, name='attend', out_shape=(jax.ShapeDtypeStr...  11.9 us

profile of v5, /device:TPU:1, one launch (start us, length us, event | category | flops | bytes accessed | tf_op | source)
XLA Modules:
  0.0 80.4 jit_solution(8059079744626248109)
XLA Ops:
  0.6 40.0 %spread_and_gather.1 = (bf16[2,4,512,128]{3,2,1,0:T(8,128)(2,1)S(1)}, bf16[4,4,2,512,128]{4,3,2,1,0:T(8,128)(2,1)S(1)}, bf16[2,512,1024]{2,1,0:T(8,128)(2,1)S(1)...) custom-call(bf16[512,512]{1,0:T(8,128)(2,1)} %q.1, bf16[512,512]{1,0:T(8,128)(2,1)} %k.1, ...), custom_call_target="tpu_custom_call" | custom-call | tf_op jit(solution)/shard_map/spread_and_gather/pallas_call | solution.py:246
  40.6 11.9 %attend.1 = (bf16[2,4,2,128,256]{4,3,2,1,0:T(8,128)(2,1)S(1)}, f32[2,4,1,512]{3,2,1,0:T(1,128)S(1)}) custom-call(s32[8,128]{1,0:T(8,128)S(1)} %get-tuple-element.10.near_table, s32[16,256]{1,0:T(8,128)S(1)} %get-tuple-element.11.lows, bf16[2,4,512,128]{3,2,1,0:T(8,128)(2,1)S(1)} %get-tuple-element.12.q, bf16[4,4,2,512,128]{4,3,2,1,0:T(8,128)(2,1)S(1)} %get-tuple-element.13.kv), custom_call_target="tpu_custom_call" | custom-call | tf_op jit(solution)/shard_map/attend/pallas_call | solution.py:379
  52.5 26.3 %return_and_project.1 = (bf16[512,1024]{1,0:T(8,128)(2,1)S(1)}, f32[4,512]{1,0:T(4,128)S(1)}) custom-call(bf16[2,4,2,128,256]{4,3,2,1,0:T(8,128)(2,1)S(1)} %get-tuple-element.14.o, f32[2,4,1,512]{3,2,1,0:T(1,128)S(1)} %get-tuple-element.15.logs, bf16[2,512,1024]{2,1,0:T(8,128)(2,1)S(1)} %get-tuple-element.16.w_near, ...), custom_call_target="tpu_custom_call" | custom-call | tf_op jit(solution)/shard_map/return_and_project/pallas_call | solution.py:560
  78.8 1.0 %copy.10 = bf16[512,1024]{1,0:T(8,128)(2,1)} copy(bf16[512,1024]{1,0:T(8,128)(2,1)S(1)} %get-tuple-element.20) | data formatting | bytes 2097152
  79.8 0.6 copy.11

commit v6 on v4

--- a/solution.py
+++ b/solution.py
@@ -151,8 +151,13 @@
             0, lengths.shape[0], walk, (jnp.int32(0), none, jnp.zeros_like(q_pos))
         )
         table[0:1, :] = where_is
-        table[1:2, :] = first
+        table[1:2, :] = first // half
         table[2:3, :] = held
+        device = where_is // 2
+        z, x, y = device // 8, device // 2 % 4, device % 2
+        p, r = z * (1 - me.core) + x * me.core, x * (1 - me.core) + z * me.core
+        table[3:4, :] = r * 8 + (y * 2 + (p + 1) // 2 % 2) * 2 + where_is % 2
+        table[4:5, :] = jnp.where(p // 2 == me.pair, 1, 0)
         lows[...] = low
 
     def spread(i, a):
@@ -296,14 +301,11 @@
             stream = jnp.where(count[n] < count[stream], n, stream)
 
         def add(key_block, filled):
-            at = table[0, key_block]
-            p, r, y = split_ctx(lax.div(at, 2), me.core)
-            slot = r * 8 + (y * 2 + pair_bit(p)) * 2 + lax.rem(at, 2)
-            work[stream, filled] = (u * blocks + key_block) * 32 + slot
-            return filled + jnp.where(lax.div(p, 2) == me.pair, 1, 0)
+            work[stream, filled] = (u * blocks + key_block) * 32 + table[3, key_block]
+            return filled + table[4, key_block]
 
         count[stream] = lax.fori_loop(
-            lax.div(table[1, block], half), block + 1, add, count[stream]
+            table[1, block], block + 1, add, count[stream]
         )
         return 0
 

time: 81.8 us -> 80.5 us (0.984)
  Pallas kernels: 79.5 us -> 78.2 us
    pallas_call x1, Pallas kernels: 10.4 us -> 9.24 us  [attend(): pl.pallas_call(attend_kernel, name='attend', out_shape=(jax.ShapeDtypeStr...]
where the time goes in v6:
time: 80.5 us; the launch traced here: 80.4 us
  Pallas kernels  78.2 us (97%)
  local copies, waits for them, and re-layouts  1.57 us (2%)
    pallas_call x1, Pallas kernels, gather(): pl.pallas_call(gather_kernel, name='spread_and_gather', out_shape=(jax.Sh...  40 us
    pallas_call x1, Pallas kernels, project(): pl.pallas_call(project_kernel, name='return_and_project', out_shape=(jax....  29 us
    pallas_call x1, Pallas kernels, attend(): pl.pallas_call(attend_kernel, name='attend', out_shape=(jax.ShapeDtypeStr...  9.24 us

profile of v6, /device:TPU:1, one launch (start us, length us, event | category | flops | bytes accessed | tf_op | source)
XLA Modules:
  0.0 80.4 jit_solution(7815750180100713299)
XLA Ops:
  0.6 40.0 %spread_and_gather.1 = (bf16[2,4,512,128]{3,2,1,0:T(8,128)(2,1)S(1)}, bf16[4,4,2,512,128]{4,3,2,1,0:T(8,128)(2,1)S(1)}, bf16[2,512,1024]{2,1,0:T(8,128)(2,1)S(1)...) custom-call(bf16[512,512]{1,0:T(8,128)(2,1)} %q.1, bf16[512,512]{1,0:T(8,128)(2,1)} %k.1, ...), custom_call_target="tpu_custom_call" | custom-call | tf_op jit(solution)/shard_map/spread_and_gather/pallas_call | solution.py:251
  40.6 9.2 %attend.1 = (bf16[2,4,4,128,128]{4,3,2,1,0:T(8,128)(2,1)S(1)}, f32[2,4,1,512]{3,2,1,0:T(1,128)S(1)}) custom-call(s32[8,128]{1,0:T(8,128)S(1)} %get-tuple-element.10.near_table, s32[16,256]{1,0:T(8,128)S(1)} %get-tuple-element.11.lows, bf16[2,4,512,128]{3,2,1,0:T(8,128)(2,1)S(1)} %get-tuple-element.12.q, bf16[4,4,2,512,128]{4,3,2,1,0:T(8,128)(2,1)S(1)} %get-tuple-element.13.kv), custom_call_target="tpu_custom_call" | custom-call | tf_op jit(solution)/shard_map/attend/pallas_call | solution.py:381
  49.9 29.0 %return_and_project.1 = (bf16[512,1024]{1,0:T(8,128)(2,1)S(1)}, f32[4,512]{1,0:T(4,128)S(1)}) custom-call(bf16[2,4,4,128,128]{4,3,2,1,0:T(8,128)(2,1)S(1)} %get-tuple-element.14.o, f32[2,4,1,512]{3,2,1,0:T(1,128)S(1)} %get-tuple-element.15.logs, bf16[2,512,1024]{2,1,0:T(8,128)(2,1)S(1)} %get-tuple-element.16.w_near, ...), custom_call_target="tpu_custom_call" | custom-call | tf_op jit(solution)/shard_map/return_and_project/pallas_call | solution.py:562
  78.8 1.0 %copy.10 = bf16[512,1024]{1,0:T(8,128)(2,1)} copy(bf16[512,1024]{1,0:T(8,128)(2,1)S(1)} %get-tuple-element.20) | data formatting | bytes 2097152
  79.8 0.6 copy.11

commit v7 on v6

--- a/solution.py
+++ b/solution.py
@@ -129,10 +129,12 @@
         lane = lax.broadcasted_iota(jnp.int32, (1, table.shape[1]), 1)
         row = lax.broadcasted_iota(jnp.int32, lows.shape, 0)
         q_pos = lax.broadcasted_iota(jnp.int32, lows.shape, 1)
+        wanted = jnp.zeros_like(lane)
         for u in range(16):
             p, y = member_place(u // 8, u // 2 % 4)
             block = layout[ctx_of(me.core, p, me.r, y) * 2 + u % 2]
             q_pos += jnp.where(row == u, block * half, 0)
+            wanted = jnp.where(lane == u, block, wanted)
 
         def place(b, state):
             where_is, held = state
@@ -157,6 +159,7 @@
         z, x, y = device // 8, device // 2 % 4, device % 2
         p, r = z * (1 - me.core) + x * me.core, x * (1 - me.core) + z * me.core
         table[3:4, :] = r * 8 + (y * 2 + (p + 1) // 2 % 2) * 2 + where_is % 2
+        table[5:6, :] = wanted
         table[4:5, :] = jnp.where(p // 2 == me.pair, 1, 0)
         lows[...] = low
 
@@ -277,7 +280,6 @@
 def attend_kernel(
     near_table, lows, q, kv, out, logs, table, work, count, top, total, summed, table_sem
 ):
-    me = Place()
     blocks = BLOCKS
     half = q.shape[2] // 2
     spare = 16
@@ -291,8 +293,7 @@
     fetch.wait()
 
     def query_block(u):
-        p, y = member_place(lax.div(u, 8), lax.rem(lax.div(u, 2), 4))
-        return table[2, ctx_of(me.core, p, me.r, y) * 2 + lax.rem(u, 2)]
+        return table[5, u]
 
     def plan(u, _):
         block = query_block(u)
@@ -325,14 +326,14 @@
         todo = []
         for n in range(STREAMS):
             code = work[n, t]
-            slot = lax.rem(code, 32)
-            key_block = lax.rem(lax.div(code, 32), blocks)
-            u = lax.div(code, 32 * blocks)
+            slot = code & 31
+            key_block = (code >> 5) & (blocks - 1)
+            u = code >> 11
             real = jnp.minimum(u, spare - 1)
-            q_rows = pl.ds(pl.multiple_of(lax.rem(real, 2) * half, half), half)
-            k_rows = pl.ds(pl.multiple_of(lax.rem(slot, 2) * half, half), half)
-            r_k, m_k = lax.div(slot, 8), lax.rem(lax.div(slot, 2), 4)
-            query = q[lax.div(real, 8), lax.rem(lax.div(real, 2), 4), q_rows, :]
+            q_rows = pl.ds(pl.multiple_of((real & 1) * half, half), half)
+            k_rows = pl.ds(pl.multiple_of((slot & 1) * half, half), half)
+            r_k, m_k = slot >> 3, (slot >> 1) & 3
+            query = q[real >> 3, (real >> 1) & 3, q_rows, :]
             key, value = kv[r_k, m_k, 0, k_rows, :], kv[r_k, m_k, 1, k_rows, :]
             q_pos = query_block(real) * half + lax.broadcasted_iota(jnp.int32, (1, half), 1)
             todo.append((u, key_block, query, key, value, q_pos, lows[pl.ds(real, 1), :]))

time: 80.5 us -> 80.4 us (level)
    pallas_call x1, Pallas kernels: 9.24 us -> 7.4 us  [attend(): pl.pallas_call(attend_kernel, name='attend', out_shape=(jax.ShapeDtypeStr...]
    pallas_call x1, Pallas kernels: 29 us -> 30.1 us  [project(): pl.pallas_call(project_kernel, name='return_and_project', out_shape=(jax....]
where the time goes in v7:
time: 80.4 us; the launch traced here: 79.6 us
  Pallas kernels  77.4 us (96%)
  local copies, waits for them, and re-layouts  1.57 us (2%)
    pallas_call x1, Pallas kernels, gather(): pl.pallas_call(gather_kernel, name='spread_and_gather', out_shape=(jax.Sh...  40 us
    pallas_call x1, Pallas kernels, project(): pl.pallas_call(project_kernel, name='return_and_project', out_shape=(jax....  30.1 us
    pallas_call x1, Pallas kernels, attend(): pl.pallas_call(attend_kernel, name='attend', out_shape=(jax.ShapeDtypeStr...  7.4 us

profile of v7, /device:TPU:1, one launch (start us, length us, event | category | flops | bytes accessed | tf_op | source)
XLA Modules:
  0.0 79.6 jit_solution(16825589483442348481)
XLA Ops:
  0.6 40.0 %spread_and_gather.1 = (bf16[2,4,512,128]{3,2,1,0:T(8,128)(2,1)S(1)}, bf16[4,4,2,512,128]{4,3,2,1,0:T(8,128)(2,1)S(1)}, bf16[2,512,1024]{2,1,0:T(8,128)(2,1)S(1)...) custom-call(bf16[512,512]{1,0:T(8,128)(2,1)} %q.1, bf16[512,512]{1,0:T(8,128)(2,1)} %k.1, ...), custom_call_target="tpu_custom_call" | custom-call | tf_op jit(solution)/shard_map/spread_and_gather/pallas_call | solution.py:254
  40.6 7.4 %attend.1 = (bf16[2,4,4,128,128]{4,3,2,1,0:T(8,128)(2,1)S(1)}, f32[2,4,1,512]{3,2,1,0:T(1,128)S(1)}) custom-call(s32[8,128]{1,0:T(8,128)S(1)} %get-tuple-element.10.near_table, s32[16,256]{1,0:T(8,128)S(1)} %get-tuple-element.11.lows, bf16[2,4,512,128]{3,2,1,0:T(8,128)(2,1)S(1)} %get-tuple-element.12.q, bf16[4,4,2,512,128]{4,3,2,1,0:T(8,128)(2,1)S(1)} %get-tuple-element.13.kv), custom_call_target="tpu_custom_call" | custom-call | tf_op jit(solution)/shard_map/attend/pallas_call | solution.py:382
  48.0 30.1 %return_and_project.1 = (bf16[512,1024]{1,0:T(8,128)(2,1)S(1)}, f32[4,512]{1,0:T(4,128)S(1)}) custom-call(bf16[2,4,4,128,128]{4,3,2,1,0:T(8,128)(2,1)S(1)} %get-tuple-element.14.o, f32[2,4,1,512]{3,2,1,0:T(1,128)S(1)} %get-tuple-element.15.logs, bf16[2,512,1024]{2,1,0:T(8,128)(2,1)S(1)} %get-tuple-element.16.w_near, ...), custom_call_target="tpu_custom_call" | custom-call | tf_op jit(solution)/shard_map/return_and_project/pallas_call | solution.py:563
  78.1 1.0 %copy.10 = bf16[512,1024]{1,0:T(8,128)(2,1)} copy(bf16[512,1024]{1,0:T(8,128)(2,1)S(1)} %get-tuple-element.20) | data formatting | bytes 2097152
  79.0 0.6 copy.11
